TPU v7x, 512 devices: a whole 4x8x8 slice. The times are simulated.
512 devices in a mesh: res: 128 (over z, y, core), crop: 4 (over x).
Axes of the slice: x: 4, y: 8, z: 8, core: 2. Of those that a mesh axis runs over, the one named last changes fastest.
Arguments:
- pair_input: bfloat16 [2560, 640, 128], P(('crop', 'res')), parts along dimension 0, may hold values from -40 to 40
- gain_in: float32 [128], replicated, may hold values from 0.5 to 1.5
- w_in: bfloat16 [128, 640], replicated, may hold values from -0.5 to 0.5
- w_out: bfloat16 [128, 128], replicated, may hold values from -0.5 to 0.5
- product_gain: float32 [128], replicated, may hold values from 0.5 to 1.5
- cotangent: bfloat16 [2560, 640, 128], P(('crop', 'res')), parts along dimension 0, may hold values from -6 to 6
Outputs:
- update: bfloat16 [2560, 640, 128], P(('crop', 'res')), parts along dimension 0
- grad_pair: bfloat16 [2560, 640, 128], P(('crop', 'res')), parts along dimension 0
- grad_w_in: float32 [512, 640], P('crop'), parts along dimension 0
- grad_w_out: float32 [512, 128], P('crop'), parts along dimension 0
- grad_gain_in: float32 [512], P('crop'), parts along dimension 0
- grad_gain_out: float32 [512], P('crop'), parts along dimension 0
There are 4 independent parts, one for each index of `crop`. A program takes and returns all parts, laid end to end along the dimension named above; an argument that names none is the same for every part. Nothing has to cross between parts.
All inputs are finite; a program needn't handle non-finite values.
Results may differ from a plain program's by a relative error of at most 0.0085.
Values may be sent and summed in bfloat16 or wider, within the bound.
A program may use at most 64 MiB of HBM per device.

v0:
```python
import jax
import jax.numpy as jnp
from jax import lax
from jax.sharding import PartitionSpec as P

EPS = 1e-05


def layer_norm_moments(value, reduce_axis):
    vf = value.astype(jnp.float32)
    center = vf - jnp.mean(vf, axis=reduce_axis, keepdims=True)
    inverse = lax.rsqrt(jnp.mean(center * center, axis=reduce_axis, keepdims=True) + EPS)
    return (center * inverse, inverse)


def layer_norm_backward(upstream, normal, inverse, reduce_axis):
    first = jnp.mean(upstream, axis=reduce_axis, keepdims=True)
    second = jnp.mean(upstream * normal, axis=reduce_axis, keepdims=True)
    return inverse * (upstream - first - normal * second)


def triangle(left_cols, right_cols):
    return jnp.einsum(
        "ick,jck->icj", left_cols, right_cols, preferred_element_type=jnp.float32
    ).astype(jnp.bfloat16)


def on_device(pair_input, gain_in, w_in, w_out, product_gain, cotangent):
    bfloat_cast = jnp.bfloat16
    fl = jnp.float32
    width = pair_input.shape[2]
    length = pair_input.shape[1]
    zhat, zinv = layer_norm_moments(pair_input, 2)
    normed = (zhat * gain_in).astype(bfloat_cast)
    factor_proj = jnp.einsum("rkd,de->rek", normed, w_in[:, : 4 * width], preferred_element_type=fl)
    gate_proj = jnp.einsum("rkd,de->rke", normed, w_in[:, 4 * width :], preferred_element_type=fl)
    p_left = factor_proj[:, 0:width]
    g_left = jax.nn.sigmoid(factor_proj[:, width : 2 * width])
    left_rows = (g_left * p_left).astype(bfloat_cast)
    p_right = factor_proj[:, 2 * width : 3 * width]
    g_right = jax.nn.sigmoid(factor_proj[:, 3 * width :])
    right_rows = (g_right * p_right).astype(bfloat_cast)
    left_cols, right_cols = (
        lax.all_to_all(left_rows, "res", split_axis=1, concat_axis=0, tiled=True),
        lax.all_to_all(right_rows, "res", split_axis=1, concat_axis=0, tiled=True),
    )
    prod_cols = triangle(left_cols, right_cols)
    triangle_product_rows = lax.all_to_all(
        prod_cols, "res", split_axis=0, concat_axis=1, tiled=True
    )
    centered_scaled_input, inverse_deviation = layer_norm_moments(triangle_product_rows, 1)
    input_normalized = (centered_scaled_input * product_gain[None, :, None]).astype(bfloat_cast)
    lin = jnp.einsum("rcj,ce->rje", input_normalized, w_out, preferred_element_type=fl)
    gate = jax.nn.sigmoid(gate_proj)
    update = (gate * lin).astype(bfloat_cast)
    upstream = cotangent.astype(fl)
    d_lin = (upstream * gate).astype(bfloat_cast)
    d_gate = (upstream * lin * gate * (1.0 - gate)).astype(bfloat_cast)
    gw_out = jnp.einsum("rcj,rje->ce", input_normalized, d_lin, preferred_element_type=fl)
    normed_gradient = jnp.einsum("rje,ce->rcj", d_lin, w_out, preferred_element_type=fl)
    product_gain_gradient = jnp.sum(normed_gradient * centered_scaled_input, axis=(0, 2))
    product_gradient = layer_norm_backward(
        normed_gradient * product_gain[None, :, None], centered_scaled_input, inverse_deviation, 1
    ).astype(bfloat_cast)
    d_prod_cols = lax.all_to_all(product_gradient, "res", split_axis=1, concat_axis=0, tiled=True)
    d_left_cols = jnp.einsum(
        "icj,jck->ick", d_prod_cols, right_cols, preferred_element_type=fl
    ).astype(bfloat_cast)
    d_right_cols = jnp.einsum(
        "icj,ick->jck", d_prod_cols, left_cols, preferred_element_type=fl
    ).astype(bfloat_cast)
    d_left, d_right = (
        lax.all_to_all(d_left_cols, "res", split_axis=0, concat_axis=1, tiled=True),
        lax.all_to_all(d_right_cols, "res", split_axis=0, concat_axis=1, tiled=True),
    )
    d_left = d_left.astype(fl)
    d_right = d_right.astype(fl)
    d_factor = jnp.concatenate(
        [
            d_left * g_left,
            d_left * p_left * g_left * (1.0 - g_left),
            d_right * g_right,
            d_right * p_right * g_right * (1.0 - g_right),
        ],
        axis=1,
    ).astype(bfloat_cast)
    gw_in = jnp.concatenate(
        [
            jnp.einsum("rkd,rek->de", normed, d_factor, preferred_element_type=fl),
            jnp.einsum("rkd,rke->de", normed, d_gate, preferred_element_type=fl),
        ],
        axis=1,
    )
    d_normed = jnp.einsum("rek,de->rkd", d_factor, w_in[:, : 4 * width], preferred_element_type=fl)
    d_normed = d_normed + jnp.einsum(
        "rke,de->rkd", d_gate, w_in[:, 4 * width :], preferred_element_type=fl
    )
    gg_in = jnp.sum(d_normed * zhat, axis=(0, 1))
    grad_pair = layer_norm_backward(d_normed * gain_in, zhat, zinv, 2).astype(bfloat_cast)
    total_in, total_out, total_gain_in, total_gain_out = lax.psum(
        (gw_in, gw_out, gg_in, product_gain_gradient), "res"
    )
    scale = 1.0 / length
    return (
        update,
        grad_pair,
        total_in * scale,
        total_out * scale,
        total_gain_in * scale,
        total_gain_out * scale,
    )


def solution(mesh):
    return jax.shard_map(
        on_device,
        mesh=mesh,
        in_specs=(
            P(("crop", "res"), None, None),
            P(),
            P(),
            P(),
            P(),
            P(("crop", "res"), None, None),
        ),
        out_specs=(
            P(("crop", "res"), None, None),
            P(("crop", "res"), None, None),
            P("crop", None),
            P("crop", None),
            P("crop"),
            P("crop"),
        ),
        check_vma=False,
    )
```

profile of v0, /device:TPU:1, one launch (start us, length us, event | category | flops | bytes accessed | tf_op | source)
XLA Modules:
  0.0 751.8 jit_solution(14681758863318959451)
XLA Ops:
  7.2 1.9 copy.44
  9.5 1.1 convolution_bitcast_fusion
  10.6 0.9 multiply_convert_fusion.3
  11.5 1.9 copy-done.1
  13.3 1.7 copy.49
  15.0 18.4 %all-to-all-start.1 = ((bf16[5,128,640]{2,0,1:T(8,128)(2,1)}), bf16[5,128,640]{2,0,1:T(8,128)(2,1)S(1)}, u32[]{:S(2)}, u32[]{:S(2)}) async-start(bf16[5,128,640]{2,0,1:T(8,128)(2,1)} %copy.49), calls=%async_computation.1 | async-start | bytes 2621440 | tf_op jit(solution)/shard_map/all_to_all | solution.py:44
  33.4 1.6 copy.48
  35.0 34.5 %all-to-all-done.1 = bf16[5,128,640]{2,0,1:T(8,128)(2,1)S(1)} async-done(((bf16[5,128,640]{2,0,1:T(8,128)(2,1)}), bf16[5,128,640]{2,0,1:T(8,128)(2,1)S(1)}, u32[]{:S(2)}, u32[]{:S(2)}) %all-to-all-start.1) | async-done | bytes 819232 | tf_op jit(solution)/shard_map/all_to_all | solution.py:44
  69.5 7.6 %all-to-all-start = ((bf16[5,128,640]{2,0,1:T(8,128)(2,1)}), bf16[5,128,640]{2,0,1:T(8,128)(2,1)S(1)}, u32[]{:S(2)}, u32[]{:S(2)}) async-start(bf16[5,128,640]{2,0,1:T(8,128)(2,1)} %copy.48), calls=%async_computation | async-start | bytes 2621440 | tf_op jit(solution)/shard_map/all_to_all | solution.py:45
  77.1 1.6 copy.50
  78.6 2.1 copy.51
  80.8 1.1 reshape.96
  81.9 31.1 %all-to-all-done = bf16[5,128,640]{2,0,1:T(8,128)(2,1)S(1)} async-done(((bf16[5,128,640]{2,0,1:T(8,128)(2,1)}), bf16[5,128,640]{2,0,1:T(8,128)(2,1)S(1)}, u32[]{:S(2)}, u32[]{:S(2)}) %all-to-all-start) | async-done | bytes 819232 | tf_op jit(solution)/shard_map/all_to_all | solution.py:45
  113.0 0.4 reshape.95
  113.4 2.3 fusion.34
  115.8 0.5 broadcast.105
  116.3 1.2 reduce.1
  117.5 0.9 copy.100
  118.5 1.2 reshape.113
  119.6 33.8 %all_to_all.72 = bf16[128,2,1600]{2,1,0:T(2,128)(2,1)S(1)} all-to-all(bf16[128,2,1600]{2,1,0:T(2,128)(2,1)S(1)} %reshape.113), channel_id=1, replica_groups=mesh['res'=128,'crop'=4] {'res'}, dimensions={0} | all-to-all | bytes 1638400 | tf_op jit(solution)/shard_map/all_to_all | solution.py:48
  153.4 2.4 reshape.114
  155.8 3.1 convert.24
  159.6 0.5 fusion.46
  160.1 0.6 copy-done.5
  160.7 3.0 fusion.16
  163.8 0.8 fusion.31
  164.6 0.3 copy-done.2
  164.9 0.5 multiply_convert_fusion
  165.4 0.5 copy.55
  165.9 42.0 %all_to_all.73 = bf16[5,128,640]{2,0,1:T(8,128)(2,1)S(1)} all-to-all(bf16[5,128,640]{2,0,1:T(8,128)(2,1)S(1)} %copy.55), channel_id=1, replica_groups=mesh['res'=128,'crop'=4] {'res'}, dimensions={1} | all-to-all | bytes 1638400 | tf_op jit(solution)/shard_map/all_to_all | solution.py:65
  207.9 1.1 copy-done.4
  209.1 1.6 copy.57
  210.7 2.2 reshape.97
  212.9 3.0 fusion.35
  215.9 2.4 reduce.2
  218.3 1.3 copy.101
  219.6 3.5 reshape.117
  223.2 7.0 all-to-all-start.4
  230.2 3.3 fusion.36
  233.5 3.0 reduce.3
  236.6 2.2 copy.102
  238.7 3.5 reshape.115
  242.3 14.9 %all-to-all-done.4 = bf16[128,2,1600]{2,1,0:T(2,128)(2,1)S(1)} async-done(((bf16[128,2,1600]{2,1,0:T(2,128)(2,1)}), bf16[128,2,1600]{2,1,0:T(2,128)(2,1)S(1)}, u32[]{:S(2)}, u32[]{:S(2)}) %all-to-all-start.4) | async-done | bytes 819232 | tf_op jit(solution)/shard_map/all_to_all | solution.py:73
  257.2 6.6 all-to-all-start.5
  263.9 2.3 convolution_bitcast_fusion.3
  266.2 2.5 fusion.48
  268.7 1.1 convolution_bitcast_fusion.2
  269.9 2.4 reshape.118
  272.3 3.1 convert.25
  275.4 15.1 %all-to-all-done.5 = bf16[128,2,1600]{2,1,0:T(2,128)(2,1)} async-done(((bf16[128,2,1600]{2,1,0:T(2,128)(2,1)}), bf16[128,2,1600]{2,1,0:T(2,128)(2,1)}, u32[]{:S(2)}, u32[]{:S(2)}) %all-to-all-start.5) | async-done | bytes 819232 | tf_op jit(solution)/shard_map/all_to_all | solution.py:74
  290.5 6.4 reshape.116
  296.9 3.1 convert.26
  300.0 3.6 fusion.27
  303.6 1.9 convolution_bitcast_fusion.1
  305.6 1.0 fusion.11
  306.6 246.2 %all-reduce = (f32[128]{0:T(128)S(1)}, f32[128]{0:T(128)S(1)}) all-reduce(f32[128]{0:T(128)S(1)} %get-tuple-element.26, f32[128]{0:T(128)S(1)} %get-tuple-element.24), channel_id=1, replica_groups=mesh['res'=128,'crop'=4] {'res'}, use_global_device_ids=true, to_apply=%region_11.0 | all-reduce | flops 256 | bytes 2048 | tf_op jit(solution)/shard_map/psum | solution.py:100
  552.8 0.5 broadcast_multiply_fusion.9
  553.4 0.5 fusion.10
  553.9 1.5 copy.66
  555.4 0.7 pad_maximum_fusion.3
  556.2 0.5 broadcast_multiply_fusion.8
  556.7 184.8 %all-reduce.4.cloned.1.call-done = (f32[128,640]{1,0:T(8,128)}, f32[128,128]{1,0:T(8,128)}) async-done(((f32[128,640]{1,0:T(8,128)}, f32[128,128]{1,0:T(8,128)}), (f32[128,640]{1,0:T(8,128)}, f32[128,128]{1,0:T(8,128)})) %all-reduce.4.cloned.1.call-update) | async-done | bytes 393232 | tf_op jit(solution)/shard_map/psum | solution.py:100
  741.5 1.7 broadcast_multiply_fusion
  743.3 1.5 broadcast_multiply_fusion.1
  (44 shorter events, 1.2 us)
Async XLA Ops:
  7.2 152.1 %copy-start = (bf16[128,128]{1,0:T(8,128)(2,1)S(1)}, bf16[128,128]{1,0:T(8,128)(2,1)}, u32[]{:S(2)}) copy-start(bf16[128,128]{1,0:T(8,128)(2,1)} %param.9) | copy-start | bytes 98308
  7.2 2.3 copy-start.16
  7.2 2.3 copy-start.12
  10.6 2.7 copy-start.1
  15.0 54.5 %all-to-all-start.1 = ((bf16[5,128,640]{2,0,1:T(8,128)(2,1)}), bf16[5,128,640]{2,0,1:T(8,128)(2,1)S(1)}, u32[]{:S(2)}, u32[]{:S(2)}) async-start(bf16[5,128,640]{2,0,1:T(8,128)(2,1)} %copy.49), calls=%async_computation.1 | async-start | bytes 2621440 | tf_op jit(solution)/shard_map/all_to_all | solution.py:44
  69.5 43.5 %all-to-all-start = ((bf16[5,128,640]{2,0,1:T(8,128)(2,1)}), bf16[5,128,640]{2,0,1:T(8,128)(2,1)S(1)}, u32[]{:S(2)}, u32[]{:S(2)}) async-start(bf16[5,128,640]{2,0,1:T(8,128)(2,1)} %copy.48), calls=%async_computation | async-start | bytes 2621440 | tf_op jit(solution)/shard_map/all_to_all | solution.py:45
  113.4 2.4 copy-start.9
  158.9 0.7 copy-start.15
  159.6 1.1 copy-start.5
  163.8 1.2 copy-start.2
  207.9 1.1 copy-start.4
  209.1 3.8 copy-start.10
  223.2 34.0 %all-to-all-start.4 = ((bf16[128,2,1600]{2,1,0:T(2,128)(2,1)}), bf16[128,2,1600]{2,1,0:T(2,128)(2,1)S(1)}, u32[]{:S(2)}, u32[]{:S(2)}) async-start(bf16[128,2,1600]{2,1,0:T(2,128)(2,1)} %reshape.117), calls=%async_computation.4 | async-start | bytes 1703936 | tf_op jit(solution)/shard_map/all_to_all | solution.py:73
  257.2 33.3 %all-to-all-start.5 = ((bf16[128,2,1600]{2,1,0:T(2,128)(2,1)}), bf16[128,2,1600]{2,1,0:T(2,128)(2,1)}, u32[]{:S(2)}, u32[]{:S(2)}) async-start(bf16[128,2,1600]{2,1,0:T(2,128)(2,1)} %reshape.115), calls=%async_computation.5 | async-start | bytes 1703936 | tf_op jit(solution)/shard_map/all_to_all | solution.py:74
  263.8 477.7 %all-reduce.4.cloned.1.call-start = ((), (), s32[]{:S(2)}) async-start(), calls=%async_computation.6 | async-start | bytes 786432 | tf_op jit(solution)/shard_map/psum | solution.py:100
  263.9 2.3 copy-start.8
  266.2 2.5 copy-start.3
  266.2 2.5 copy-start.6
  303.6 2.0 copy-start.7
  303.6 2.0 copy-start.13
  553.9 1.6 copy-start.11
  553.9 1.6 copy-start.14
Sparse Core Ops, SparseCore 0:
  556.3 185.1 all-reduce.3
where the time goes:
time: 759 us; the launch traced here: 752 us
  blocking collectives  322 us (42%)
  waiting for transfers between devices  280 us (37%)
  local copies, waits for them, and re-layouts  44.9 us (6%)
  starting transfers between devices  39.6 us (5%)
  other arithmetic  27.1 us (4%)
  matrix products  23.1 us (3%)
  between operations  14.6 us (2%)
    psum x1, blocking collectives, on_device(): lax.psum((gw_in, gw_out, gg_in, product_gain_gradient), 'res')  246 us
    psum x1, waiting for transfers between devices, on_device(): lax.psum((gw_in, gw_out, gg_in, product_gain_gradient), 'res')  185 us
    all_to_all x1, blocking collectives, on_device(): lax.all_to_all(product_gradient, 'res', split_axis=1, concat_axis=0, tile...  42 us
    all_to_all x1, waiting for transfers between devices, on_device(): lax.all_to_all(left_rows, 'res', split_axis=1, concat_axis=0, tiled=True)  34.5 us
    all_to_all x1, blocking collectives, on_device(): lax.all_to_all(prod_cols, 'res', split_axis=0, concat_axis=1, tiled=True)  33.8 us
    unnamed x45, local copies, waits for them, and re-layouts  31.6 us
    all_to_all x1, waiting for transfers between devices, on_device(): lax.all_to_all(right_rows, 'res', split_axis=1, concat_axis=0, tiled=True)  31.1 us
    all_to_all x1, starting transfers between devices, on_device(): lax.all_to_all(left_rows, 'res', split_axis=1, concat_axis=0, tiled=True)  18.4 us
  transfers between devices with their start and end apart: 5, of which 5 were waited for; matrix products, arithmetic and copies ran while one was open for 4% of the time, Pallas kernels for 0%

commit v1 on v0

v1 whole, which is shorter than its diff:
```python
import functools

import jax
import jax.numpy as jnp
from jax import lax
from jax.experimental import pallas as pl
from jax.experimental.pallas import tpu as pltpu
from jax.sharding import PartitionSpec as P

EPS = 1e-05
FL = jnp.float32
BF = jnp.bfloat16
C = 128
PIECE = 32
GROWS = 16


def dot(a, b, dims=((1,), (0,))):
    return lax.dot_general(a, b, (dims, ((), ())), preferred_element_type=FL)


NT = ((1,), (1,))
TN = ((0,), (0,))


def sigmoid(x):
    return jax.nn.sigmoid(x)


def kernel(
    parts, rows, length,
    z_ref, gain_in_ref, w_in_ref, w_out_ref, gain_out_ref, cot_ref,
    upd_ref, gp_ref, gwi_ref, gwo_ref, gains_ref,
    send, recv, gsend, grecv, bsend, brecv, packed, opened, natural,
    left_m, right_m, dprod_m,
    zhat, zinv, normed, p_l, s_l, p_r, s_r, s_g, cot_t, upd_t, xn, d_lin, d_proj,
    w_in_t, w_out_t, gain_in_c, gain_out_c, grads,
    send_sem, recv_sem, gsend_sem, grecv_sem, bsend_sem, brecv_sem,
):
    tiles = length // C
    owners = gsend.shape[0]
    me = lax.axis_index("res")

    barrier = pltpu.get_barrier_semaphore()

    def peer(step):
        return lax.rem(me + lax.rem(step * 37, parts), parts)

    def greet(step, carry):
        pl.semaphore_signal(
            barrier, inc=1, device_id={"res": peer(step)}, device_id_type=pl.DeviceIdType.MESH
        )
        return carry

    lax.fori_loop(1, parts, greet, 0)

    def copy_to(stage, to):
        return pltpu.make_async_remote_copy(
            src_ref=send.at[stage, to],
            dst_ref=recv.at[stage, me],
            send_sem=send_sem.at[stage],
            recv_sem=recv_sem.at[stage],
            device_id={"res": to},
            device_id_type=pl.DeviceIdType.MESH,
        )

    def all_pieces(stage):
        return pltpu.make_async_remote_copy(
            src_ref=send.at[stage, pl.ds(0, parts - 1)],
            dst_ref=recv.at[stage, pl.ds(0, parts - 1)],
            send_sem=send_sem.at[stage],
            recv_sem=recv_sem.at[stage],
            device_id={"res": peer(1)},
            device_id_type=pl.DeviceIdType.MESH,
        )

    def slab(row, tile):
        return pl.ds(row * tiles + tile, parts, stride=PIECE)

    def pack(row, value):
        for tile in range(tiles):
            packed[slab(row, tile), :] = value[:, tile * C : (tile + 1) * C]

    def unpack(row):
        return jnp.concatenate([opened[slab(row, tile), :] for tile in range(tiles)], axis=1)

    def send_packed(stage):
        send[stage] = packed[...].astype(BF).reshape(parts, PIECE, C)

        def start(step, carry):
            copy_to(stage, peer(step)).start()
            return carry

        lax.fori_loop(1, parts, start, 0)
        recv[stage, me] = send[stage, me]

    def receive(stage):
        all_pieces(stage).wait_recv()
        opened[...] = recv[stage].reshape(parts * PIECE, C).astype(FL)

    def square(value):
        return jnp.transpose(value.astype(FL))

    eye = (
        lax.broadcasted_iota(jnp.int32, (C, C), 0) == lax.broadcasted_iota(jnp.int32, (C, C), 1)
    ).astype(BF)
    for block in range(5):
        w_in_t[block * C : (block + 1) * C, :] = square(
            w_in_ref[:, block * C : (block + 1) * C]
        ).astype(BF)
    w_out_t[...] = square(w_out_ref[...]).astype(BF)
    gain_in_c[...] = square(jnp.broadcast_to(gain_in_ref[...], (C, C)))
    gain_out_c[...] = square(jnp.broadcast_to(gain_out_ref[...], (C, C)))
    packed[...] = jnp.zeros(packed.shape, FL)

    for row in range(rows):
        zt = dot(eye, z_ref[row], NT)
        center = zt - jnp.mean(zt, axis=0, keepdims=True)
        inverse = lax.rsqrt(jnp.mean(center * center, axis=0, keepdims=True) + EPS)
        zh = center * inverse
        zhat[row] = zh
        zinv[row] = inverse
        normed[row] = (zh * gain_in_c[:, :1]).astype(BF)
        proj = dot(w_in_t[: 2 * C, :], normed[row])
        s_l[row] = sigmoid(proj[C:])
        p_l[row] = proj[:C]
        pack(row, p_l[row] * s_l[row])
    pl.semaphore_wait(barrier, parts - 1)
    send_packed(0)
    for row in range(rows):
        proj = dot(w_in_t[2 * C : 4 * C, :], normed[row])
        s_r[row] = sigmoid(proj[C:])
        p_r[row] = proj[:C]
        pack(row, p_r[row] * s_r[row])
    send_packed(1)
    for row in range(rows):
        s_g[row] = sigmoid(dot(w_in_t[4 * C :, :], normed[row]))
        cot_t[row] = dot(eye, cot_ref[row], NT)

    receive(0)
    for row in range(rows):
        left_m[row * parts : (row + 1) * parts, :] = unpack(row).astype(BF)
    receive(1)
    for tile in range(tiles):
        for row in range(rows):
            natural[tile, pl.ds(row, parts, stride=rows), :] = opened[slab(row, tile), :]
        right_m[:, tile * C : (tile + 1) * C] = natural[tile].astype(BF)
    for row in range(rows):
        pack(row, dot(left_m[row * parts : (row + 1) * parts, :], right_m[...], NT))
    send_packed(2)

    receive(2)
    gg_out = jnp.zeros((C, C), FL)
    for row in range(rows):
        prod = unpack(row)
        center = prod - jnp.mean(prod, axis=0, keepdims=True)
        inverse = lax.rsqrt(jnp.mean(center * center, axis=0, keepdims=True) + EPS)
        xh = center * inverse
        xn[row] = (xh * gain_out_c[:, :1]).astype(BF)
        lin = dot(w_out_t[...], xn[row])
        s = s_g[row]
        upd_t[row] = s * lin
        g = cot_t[row]
        d_lin[row] = (g * s).astype(BF)
        d_proj[row, 4 * C :, :] = (g * lin * s * (1.0 - s)).astype(BF)
        d_xn = dot(w_out_ref[...], d_lin[row])
        both = d_xn * xh
        for tile in range(tiles):
            gg_out = gg_out + both[:, tile * C : (tile + 1) * C]
        h = d_xn * gain_out_c[:, :1]
        first = jnp.mean(h, axis=0, keepdims=True)
        second = jnp.mean(h * xh, axis=0, keepdims=True)
        pack(row, inverse * (h - first - xh * second))
    send_packed(3)
    for row in range(rows):
        for tile in range(tiles):
            upd_ref[row, tile * C : (tile + 1) * C, :] = jnp.transpose(
                upd_t[row, :, tile * C : (tile + 1) * C]
            ).astype(BF)
    gw = jnp.zeros((C, C), FL)
    gw_gate = jnp.zeros((C, C), FL)
    for row in range(rows):
        gw = gw + dot(xn[row], d_lin[row], NT)
        gw_gate = gw_gate + dot(normed[row], d_proj[row, 4 * C :, :], NT)
    grads[4 * C : 5 * C, :] = gw_gate
    grads[5 * C : 6 * C, :] = gw
    grads[6 * C :, :] = jnp.zeros((GROWS, C), FL)
    grads[6 * C + 1 : 6 * C + 2, :] = jnp.sum(jnp.transpose(gg_out), axis=0, keepdims=True)

    receive(3)
    for row in range(rows):
        dprod_m[row * parts : (row + 1) * parts, :] = unpack(row).astype(BF)
    for row in range(rows):
        pack(row, dot(dprod_m[row * parts : (row + 1) * parts, :], right_m[...]))
    send_packed(4)
    for tile in range(tiles):
        part = dot(dprod_m[:, tile * C : (tile + 1) * C], left_m[...], TN)
        for across in range(tiles):
            natural[across, tile * C : (tile + 1) * C, :] = part[:, across * C : (across + 1) * C]
    for row in range(rows):
        for tile in range(tiles):
            packed[slab(row, tile), :] = natural[tile, pl.ds(row, parts, stride=rows), :]
    send_packed(5)

    for side, p_ref, s_ref in ((0, p_l, s_l), (1, p_r, s_r)):
        receive(4 + side)
        base = side * 2 * C
        total = jnp.zeros((C, 2 * C), FL)
        for row in range(rows):
            d = unpack(row)
            s = s_ref[row]
            d_proj[row, base : base + C, :] = (d * s).astype(BF)
            d_proj[row, base + C : base + 2 * C, :] = (d * p_ref[row] * s * (1.0 - s)).astype(BF)
            total = total + dot(normed[row], d_proj[row, base : base + 2 * C, :], NT)
        grads[base : base + C, :] = total[:, :C]
        grads[base + C : base + 2 * C, :] = total[:, C:]

    gg_in = jnp.zeros((C, C), FL)
    for row in range(rows):
        d_normed = dot(w_in_ref[...], d_proj[row])
        p_l[row] = d_normed
        both = d_normed * zhat[row]
        for tile in range(tiles):
            gg_in = gg_in + both[:, tile * C : (tile + 1) * C]
    grads[6 * C : 6 * C + 1, :] = jnp.sum(jnp.transpose(gg_in), axis=0, keepdims=True)
    gsend[...] = grads[...].astype(BF).reshape(owners, GROWS, C)

    chip = lax.div(me, 2)
    own = jnp.logical_and(lax.rem(me, 2) == 0, chip < owners)

    def gcopy(q):
        return pltpu.make_async_remote_copy(
            src_ref=gsend.at[q],
            dst_ref=grecv.at[me],
            send_sem=gsend_sem,
            recv_sem=grecv_sem,
            device_id={"res": 2 * q},
            device_id_type=pl.DeviceIdType.MESH,
        )

    def gstart(step, carry):
        q = lax.rem(chip + step, owners)

        @pl.when(2 * q != me)
        def _():
            gcopy(q).start()

        return carry

    lax.fori_loop(0, owners, gstart, 0)

    @pl.when(own)
    def _():
        grecv[me] = gsend[chip]

    for row in range(rows):
        zh = zhat[row]
        h = p_l[row] * gain_in_c[:, :1]
        first = jnp.mean(h, axis=0, keepdims=True)
        second = jnp.mean(h * zh, axis=0, keepdims=True)
        out = zinv[row] * (h - first - zh * second)
        for tile in range(tiles):
            gp_ref[row, tile * C : (tile + 1) * C, :] = jnp.transpose(
                out[:, tile * C : (tile + 1) * C]
            ).astype(BF)

    def gall(dst, recv_on, count, src, send_on):
        return pltpu.make_async_remote_copy(
            src_ref=src.at[pl.ds(0, count)],
            dst_ref=dst.at[pl.ds(0, count)],
            send_sem=send_on,
            recv_sem=recv_on,
            device_id={"res": peer(1)},
            device_id_type=pl.DeviceIdType.MESH,
        )

    @pl.when(own)
    def _():
        gall(grecv, grecv_sem, parts - 1, grecv, gsend_sem).wait_recv()
        total = jnp.sum(grecv[...].astype(FL), axis=0)
        bsend[...] = (total * (1.0 / length)).astype(BF)

        def bstart(step, carry):
            pltpu.make_async_remote_copy(
                src_ref=bsend,
                dst_ref=brecv.at[chip],
                send_sem=bsend_sem,
                recv_sem=brecv_sem,
                device_id={"res": peer(step)},
                device_id_type=pl.DeviceIdType.MESH,
            ).start()
            return carry

        lax.fori_loop(1, parts, bstart, 0)
        brecv[chip] = bsend[...]
        gall(brecv, brecv_sem, owners - 1, brecv, bsend_sem).wait_recv()
        gall(gsend, gsend_sem, owners - 1, gsend, gsend_sem).wait_send()
        gall(grecv, grecv_sem, parts - 1, grecv, bsend_sem).wait_send()

    @pl.when(jnp.logical_not(own))
    def _():
        gall(brecv, brecv_sem, owners, brecv, bsend_sem).wait_recv()
        gall(gsend, gsend_sem, owners, gsend, gsend_sem).wait_send()

    total = brecv[...].astype(FL).reshape(owners * GROWS, C)
    for block in range(5):
        gwi_ref[:, block * C : (block + 1) * C] = total[block * C : (block + 1) * C]
    gwo_ref[...] = total[5 * C : 6 * C]
    gains_ref[...] = total[6 * C : 6 * C + 8]
    for stage in range(6):
        all_pieces(stage).wait_send()


def on_device(pair_input, gain_in, w_in, w_out, product_gain, cotangent):
    rows, length, width = pair_input.shape
    parts = lax.axis_size("res")
    owners = (6 * C) // GROWS + 1
    held = (rows, C, length)
    vmem = pl.BlockSpec(memory_space=pltpu.VMEM)
    sem = pltpu.SemaphoreType.DMA
    upd, gp, gwi, gwo, gains = pl.pallas_call(
        functools.partial(kernel, parts, rows, length),
        out_shape=(
            jax.ShapeDtypeStruct(pair_input.shape, BF),
            jax.ShapeDtypeStruct(pair_input.shape, BF),
            jax.ShapeDtypeStruct(w_in.shape, FL),
            jax.ShapeDtypeStruct(w_out.shape, FL),
            jax.ShapeDtypeStruct((8, C), FL),
        ),
        in_specs=[vmem] * 6,
        out_specs=[vmem] * 5,
        scratch_shapes=[
            pltpu.VMEM((6, parts, PIECE, C), BF),
            pltpu.VMEM((6, parts, PIECE, C), BF),
            pltpu.VMEM((owners, GROWS, C), BF),
            pltpu.VMEM((parts, GROWS, C), BF),
            pltpu.VMEM((GROWS, C), BF),
            pltpu.VMEM((owners, GROWS, C), BF),
            pltpu.VMEM((parts * PIECE, C), FL),
            pltpu.VMEM((parts * PIECE, C), FL),
            pltpu.VMEM((length // C, length, C), FL),
            pltpu.VMEM((length, length), BF),
            pltpu.VMEM((length, length), BF),
            pltpu.VMEM((length, length), BF),
            pltpu.VMEM(held, FL),
            pltpu.VMEM((rows, 1, length), FL),
            pltpu.VMEM(held, BF),
            pltpu.VMEM(held, FL),
            pltpu.VMEM(held, FL),
            pltpu.VMEM(held, FL),
            pltpu.VMEM(held, FL),
            pltpu.VMEM(held, FL),
            pltpu.VMEM(held, FL),
            pltpu.VMEM(held, FL),
            pltpu.VMEM(held, BF),
            pltpu.VMEM(held, BF),
            pltpu.VMEM((rows, 5 * C, length), BF),
            pltpu.VMEM((5 * C, C), BF),
            pltpu.VMEM((C, C), BF),
            pltpu.VMEM((C, C), FL),
            pltpu.VMEM((C, C), FL),
            pltpu.VMEM((owners * GROWS, C), FL),
            sem((6,)),
            sem((6,)),
            sem,
            sem,
            sem,
            sem,
        ],
        compiler_params=pltpu.CompilerParams(
            collective_id=0, has_side_effects=True, vmem_limit_bytes=58 * 2**20
        ),
    )(pair_input, gain_in.reshape(1, C), w_in, w_out, product_gain.reshape(1, C), cotangent)
    return upd, gp, gwi, gwo, gains[0], gains[1]


def solution(mesh):
    return jax.shard_map(
        on_device,
        mesh=mesh,
        in_specs=(
            P(("crop", "res"), None, None),
            P(),
            P(),
            P(),
            P(),
            P(("crop", "res"), None, None),
        ),
        out_specs=(
            P(("crop", "res"), None, None),
            P(("crop", "res"), None, None),
            P("crop", None),
            P("crop", None),
            P("crop"),
            P("crop"),
        ),
        check_vma=False,
    )
```

time: 759 us -> 217 us (0.29)
  blocking collectives: 322 us -> 0 us
  waiting for transfers between devices: 280 us -> 0 us
  Pallas kernels: 0 us -> 210 us
  starting transfers between devices: 39.6 us -> 0 us
  local copies, waits for them, and re-layouts: 44.9 us -> 6.09 us
  other arithmetic: 27.1 us -> 0 us
  matrix products: 23.1 us -> 0 us
  between operations: 14.6 us -> 0.65 us
    psum x1 -> x0, blocking collectives: 246 us -> none  [on_device(): lax.psum((gw_in, gw_out, gg_in, product_gain_gradient), 'res')]
    pallas_call x0 -> x1, Pallas kernels: none -> 210 us  [on_device(): pl.pallas_call(functools.partial(kernel, parts, rows, length), out_shape=...]
    psum x1 -> x0, waiting for transfers between devices: 185 us -> none  [on_device(): lax.psum((gw_in, gw_out, gg_in, product_gain_gradient), 'res')]
    all_to_all x4 -> x0, waiting for transfers between devices: 95.7 us -> none  [the longest x1 34.5 us: on_device(): lax.all_to_all(left_rows, 'res', split_axis=1, concat_axis=0, tiled=True)]
    all_to_all x2 -> x0, blocking collectives: 75.8 us -> none  [the longest x1 42 us: on_device(): lax.all_to_all(product_gradient, 'res', split_axis=1, concat_axis=0, tile...]
    all_to_all x4 -> x0, starting transfers between devices: 39.6 us -> none  [the longest x1 18.4 us: on_device(): lax.all_to_all(left_rows, 'res', split_axis=1, concat_axis=0, tiled=True)]
    unnamed x45 -> x10, local copies, waits for them, and re-layouts: 31.6 us -> 4.82 us
    dot_general x12 -> x0, matrix products: 23.1 us -> none  [the longest x1 3.35 us: on_device(): jnp.einsum('icj,ick->jck', d_prod_cols, left_cols, preferred_element_type...]
  transfers between devices with their start and end apart: 5 -> 0, of which waited for: 5 -> 0; matrix products, arithmetic and copies ran while one was open for 4% -> 0% of each run, Pallas kernels for 0% -> 0%
where the time goes in v1:
time: 217 us; the launch traced here: 216 us
  Pallas kernels  210 us (97%)
  local copies, waits for them, and re-layouts  6.09 us (3%)
    pallas_call x1, Pallas kernels, on_device(): pl.pallas_call(functools.partial(kernel, parts, rows, length), out_shape=...  210 us
    unnamed x10, local copies, waits for them, and re-layouts  4.82 us

profile of v1, /device:TPU:1, one launch (start us, length us, event | category | flops | bytes accessed | tf_op | source)
XLA Modules:
  0.0 216.3 jit_solution(1454423708701483122)
XLA Ops:
  0.6 209.6 %shard_map.109 = (bf16[5,640,128]{2,1,0:T(8,128)(2,1)}, bf16[5,640,128]{2,1,0:T(8,128)(2,1)}, f32[128,640]{1,0:T(8,128)}, f32[128,128]{1,0:T(8,128)}, f32[8,128]{1,0:T(8,128)}) custom-call(bf16[5,640,128]{2,1,0:T(8,128)(2,1)} %z_ref.1, f32[1,128]{1,0:T(1,128)} %bitcast.6, bf16[128,640]{1,0:T(8,128)(2,1)} %w_in_ref.1, bf16[128,128]{1,0:T(8,128)(2,1)} %w_out_ref.1, ...), custom_call_target="tpu_custom_call" | custom-call | tf_op jit(solution)/shard_map/pallas_call | solution.py:321
  210.2 1.3 slice_bitcast_fusion
  211.5 0.0 copy-start
  211.5 2.2 %copy.16 = bf16[5,640,128]{2,1,0:T(8,128)(2,1)} copy(bf16[5,640,128]{2,1,0:T(8,128)(2,1)} %get-tuple-element.24) | data formatting | bytes 1638400
  213.7 0.0 copy-done
  213.7 0.0 copy-start.1
  213.7 0.9 copy.17
  214.6 0.3 copy-done.1
  214.8 0.0 copy-start.2
  214.9 0.7 copy.18
  215.6 0.1 copy-done.2
  215.7 0.6 copy.19
Async XLA Ops:
  211.5 2.2 %copy-start = (bf16[5,640,128]{2,1,0:T(8,128)(2,1)S(1)}, bf16[5,640,128]{2,1,0:T(8,128)(2,1)}, u32[]{:S(2)}) copy-start(bf16[5,640,128]{2,1,0:T(8,128)(2,1)} %get-tuple-element.25) | copy-start | bytes 2457604
  213.7 1.2 copy-start.1
  214.8 0.9 copy-start.2

commit v2 on v0

v2 whole, which is shorter than its diff:
```python
import functools

import jax
import jax.numpy as jnp
from jax import lax
from jax.experimental import pallas as pl
from jax.experimental.pallas import tpu as pltpu
from jax.sharding import PartitionSpec as P

EPS = 1e-05
FL = jnp.float32
BF = jnp.bfloat16
C = 128
LINE = 8
GROUP = 2 * LINE
GROWS = 16
SIDE = 7
ROUND = (1, 7, 2, 6, 3, 5, 4)
CHUNKS = ((0, 2), (2, 3))


def dot(a, b, dims=((1,), (0,))):
    return lax.dot_general(a, b, (dims, ((), ())), preferred_element_type=FL)


NT = ((1,), (1,))


def padded(count, tiles):
    return -(-(LINE * count * tiles) // 16) * 16


def sigmoid(x):
    return jax.nn.sigmoid(x)


def kernel(
    rows, length,
    z_ref, gain_in_ref, w_in_ref, w_out_ref, gain_out_ref, cot_ref,
    upd_ref, gp_ref, gwi_ref, gwo_ref, gains_ref,
    send1, recv1, send2, recv2, mixed,
    g_send, g_recv, h_send, h_recv, o_send, c_recv, d_recv,
    left_m, right_m, dprod_m, turned_m, order, order_t, wide,
    zhat, zinv, normed, p_l, s_l, p_r, s_r, s_g, cot_t, upd_t, xn, d_lin, d_proj,
    w_in_t, w_in_p, w_out_t, w_out_p, gain_in_c, gain_out_c, perm, grads,
    send_sem1, recv_sem1, send_sem2, recv_sem2, g_sems,
):
    tiles = length // C

    def sizes(chunk):
        first, count = CHUNKS[chunk]
        start = 0 if chunk == 0 else padded(CHUNKS[0][1], tiles)
        base = 0 if chunk == 0 else LINE * GROUP * CHUNKS[0][1]
        return first, count, start, padded(count, tiles), LINE * count, base

    me = lax.axis_index("res")
    z = me // GROUP
    y = (me // 2) % LINE
    core = me % 2
    a = y + core * (z - y)
    b = z + core * (y - z)
    step_a = 2 + (GROUP - 2) * core
    step_b = GROUP - (GROUP - 2) * core

    def device(at_a, at_b, at_core):
        return at_a * step_a + at_b * step_b + at_core

    def remote(src, dst, on_send, on_recv, to):
        return pltpu.make_async_remote_copy(
            src_ref=src,
            dst_ref=dst,
            send_sem=on_send,
            recv_sem=on_recv,
            device_id={"res": to},
            device_id_type=pl.DeviceIdType.MESH,
        )

    other = device(a, b, 1 - core)
    barrier = pltpu.get_barrier_semaphore()

    def greet(to):
        pl.semaphore_signal(
            barrier, inc=1, device_id={"res": to}, device_id_type=pl.DeviceIdType.MESH
        )

    greet(other)
    for t in ROUND:
        for at_core in (0, 1):
            greet(device((a + t) % LINE, b, at_core))
            greet(device(a, (b + t) % LINE, at_core))

    def send_rows(stage, chunk):
        first, count = CHUNKS[chunk]
        part = pl.ds(first, count)
        for t in ROUND:
            at_a = (a + t) % LINE
            remote(
                send1.at[stage, at_a, part],
                recv1.at[stage, a, part],
                send_sem1.at[stage, chunk],
                recv_sem1.at[stage, chunk],
                device(at_a, b, core),
            ).start()
        recv1[stage, a, part] = send1[stage, a, part]

    def all_a(stage, chunk):
        first, count = CHUNKS[chunk]
        return remote(
            send1.at[stage, pl.ds(0, LINE - 1), pl.ds(first, count)],
            recv1.at[stage, pl.ds(0, LINE - 1), pl.ds(first, count)],
            send_sem1.at[stage, chunk],
            recv_sem1.at[stage, chunk],
            other,
        )

    def all_b(stage, chunk):
        _, _, start, piece, _, _ = sizes(chunk)
        return remote(
            send2.at[stage, pl.ds(0, GROUP - 1), pl.ds(start, piece)],
            recv2.at[stage, pl.ds(0, GROUP - 1), pl.ds(start, piece)],
            send_sem2.at[stage, chunk],
            recv_sem2.at[stage, chunk],
            other,
        )

    def place(stage, row, value):
        value = value.astype(BF)
        for at in range(LINE):
            send1[stage, at, row] = value[at * GROUP : (at + 1) * GROUP]

    def relay_rows(stage, chunk):
        first, count, start, piece, _, _ = sizes(chunk)
        part = pl.ds(start, piece)
        stride = piece + 1
        all_a(stage, chunk).wait_recv()
        for at in range(LINE):
            for row in range(count):
                block = recv1[stage, at, first + row].astype(FL)
                for tile in range(tiles):
                    where = (at * count + row) * tiles + tile
                    mixed[pl.ds(where, GROUP, stride=stride), :] = block[
                        :, tile * C : (tile + 1) * C
                    ]
        for q in range(GROUP):
            send2[stage, q, part] = mixed[q * stride : q * stride + piece, :].astype(BF)
        mine = b * 2 + core
        for t in (0,) + ROUND:
            at_b = (b + t) % LINE
            for turn in (0, 1):
                if t == 0 and turn == 0:
                    continue
                at_core = (core + turn) % 2
                remote(
                    send2.at[stage, at_b * 2 + at_core, part],
                    recv2.at[stage, mine, part],
                    send_sem2.at[stage, chunk],
                    recv_sem2.at[stage, chunk],
                    device(a, at_b, at_core),
                ).start()
        recv2[stage, mine, part] = send2[stage, mine, part]

    def take_channel(stage, chunk, into):
        first, count, start, piece, lot, base = sizes(chunk)
        all_b(stage, chunk).wait_recv()
        for slot in range(GROUP):
            mixed[slot * piece : (slot + 1) * piece, :] = recv2[
                stage, slot, start : start + piece
            ].astype(FL)
        for at in range(LINE):
            top = base + at * 2 * lot
            for tile in range(tiles):
                both = [
                    mixed[pl.ds((at * 2 + k) * piece + tile, lot, stride=tiles), :]
                    for k in (0, 1)
                ]
                into[top : top + 2 * lot, tile * C : (tile + 1) * C] = (
                    jnp.concatenate(both, axis=0).astype(BF)
                )

    def of(factor, chunk):
        _, _, _, _, lot, base = sizes(chunk)
        return factor[base : base + GROUP * lot, :]

    def send_channel(stage, chunk, whole):
        _, _, start, piece, lot, _ = sizes(chunk)
        slab = pl.ds(start, piece)
        wide[: GROUP * lot, :] = whole
        for t in (0,) + ROUND:
            at_b = (b + t) % LINE
            part = wide[pl.ds(pl.multiple_of(at_b * 2 * lot, GROUP), 2 * lot), :]
            for k in (0, 1):
                for tile in range(tiles):
                    mixed[pl.ds(k * piece + tile, lot, stride=tiles), :] = part[
                        k * lot : (k + 1) * lot, tile * C : (tile + 1) * C
                    ]
            for k in (0, 1):
                send2[stage, at_b * 2 + k, slab] = mixed[k * piece : (k + 1) * piece, :].astype(BF)
                to = (at_b * GROUP + y * 2) if k == 0 else (z * GROUP + at_b * 2 + 1)
                copy = remote(
                    send2.at[stage, at_b * 2 + k, slab],
                    recv2.at[stage, (z if k == 0 else y) * 2 + core, slab],
                    send_sem2.at[stage, chunk],
                    recv_sem2.at[stage, chunk],
                    to,
                )
                if t == 0:

                    @pl.when(core == k)
                    def _():
                        recv2[stage, at_b * 2 + k, slab] = send2[stage, at_b * 2 + k, slab]

                    @pl.when(core != k)
                    def _():
                        copy.start()

                else:
                    copy.start()

    def relay_channel(stage, chunk):
        first, count, start, piece, _, _ = sizes(chunk)
        stride = piece + 1
        all_b(stage, chunk).wait_recv()
        for q in range(GROUP):
            mixed[q * stride : q * stride + piece, :] = recv2[
                stage, q, start : start + piece
            ].astype(FL)
        for at in range(LINE):
            for row in range(count):
                for tile in range(tiles):
                    where = (at * count + row) * tiles + tile
                    send1[stage, at, first + row, :, tile * C : (tile + 1) * C] = mixed[
                        pl.ds(where, GROUP, stride=stride), :
                    ].astype(BF)
        send_rows(stage, chunk)

    def take_row(stage, row):
        return jnp.concatenate([recv1[stage, at, row] for at in range(LINE)], axis=0).astype(FL)

    def chunk_rows(chunk):
        first, count = CHUNKS[chunk]
        return range(first, first + count)

    def iota(shape, dim):
        return lax.broadcasted_iota(jnp.int32, shape, dim)

    eye = (iota((C, C), 0) == iota((C, C), 1)).astype(BF)
    q = iota((C, C), 0)
    home = (q >> 4) * step_a + ((q >> 1) & 7) * step_b + (q & 1)
    perm_f = (home == iota((C, C), 1)).astype(FL)
    perm[...] = perm_f.astype(BF)
    for block in range(5):
        sort = perm[...] if block < 4 else eye
        cols = slice(block * C, (block + 1) * C)
        w_in_t[cols, :] = dot(sort, w_in_ref[:, cols], NT).astype(BF)
        w_in_p[:, cols] = dot(w_in_ref[:, cols], sort, NT).astype(BF)
    w_out_p[...] = dot(perm[...], w_out_ref[...]).astype(BF)
    w_out_t[...] = jnp.transpose(dot(perm[...], w_out_ref[...])).astype(BF)
    gain_in_c[...] = jnp.transpose(jnp.broadcast_to(gain_in_ref[...], (C, C)))
    gain_out_c[...] = jnp.broadcast_to(
        jnp.sum(perm_f * gain_out_ref[...], axis=1, keepdims=True), (C, C)
    )
    mixed[...] = jnp.zeros(mixed.shape, FL)

    for chunk in (0, 1):
        for row in chunk_rows(chunk):
            zt = dot(eye, z_ref[row], NT)
            center = zt - jnp.mean(zt, axis=0, keepdims=True)
            inverse = lax.rsqrt(jnp.mean(center * center, axis=0, keepdims=True) + EPS)
            zh = center * inverse
            zhat[row] = zh
            zinv[row] = inverse
            normed[row] = (zh * gain_in_c[:, :1]).astype(BF)
            proj = dot(w_in_t[: 2 * C, :], normed[row])
            s_l[row] = sigmoid(proj[C:])
            p_l[row] = proj[:C]
            place(0, row, p_l[row] * s_l[row])
        if chunk == 0:
            pl.semaphore_wait(barrier, 4 * LINE - 3)
        send_rows(0, chunk)
    for chunk in (0, 1):
        for row in chunk_rows(chunk):
            proj = dot(w_in_t[2 * C : 4 * C, :], normed[row])
            s_r[row] = sigmoid(proj[C:])
            p_r[row] = proj[:C]
            place(1, row, p_r[row] * s_r[row])
        send_rows(1, chunk)
    relay_rows(0, 0)
    relay_rows(0, 1)
    for row in range(rows):
        s_g[row] = sigmoid(dot(w_in_t[4 * C :, :], normed[row]))
    relay_rows(1, 0)
    relay_rows(1, 1)
    for row in range(rows):
        cot_t[row] = dot(eye, cot_ref[row], NT)

    def natural(p):
        split = LINE * GROUP * CHUNKS[0][1]
        second = p >= split
        count = jnp.where(second, float(CHUNKS[1][1]), float(CHUNKS[0][1]))
        pf = p.astype(FL) + 0.5 - jnp.where(second, float(split), 0.0)
        at_b = jnp.floor(pf / (count * GROUP))
        pf = pf - at_b * (count * GROUP)
        at_core = jnp.floor(pf / (count * LINE))
        pf = pf - at_core * (count * LINE)
        at_a = jnp.floor(pf / count)
        row = pf - 0.5 - at_a * count + jnp.where(second, float(CHUNKS[1][0]), 0.0)
        at_z = at_b + at_core * (at_a - at_b)
        at_y = at_a + at_core * (at_b - at_a)
        return ((at_z * GROUP + at_y * 2 + at_core) * rows + row + 0.5).astype(jnp.int32)

    order[...] = (iota((length, length), 0) == natural(iota((1, length), 1))).astype(FL).astype(BF)
    order_t[...] = (
        (iota((length, length), 1) == natural(iota((length, 1), 0))).astype(FL).astype(BF)
    )

    take_channel(0, 0, left_m)
    take_channel(0, 1, left_m)
    take_channel(1, 0, turned_m)
    take_channel(1, 1, turned_m)
    right_m[...] = dot(order[...], turned_m[...]).astype(BF)
    for chunk in (0, 1):
        send_channel(2, chunk, dot(of(left_m, chunk), right_m[...], NT))
    for chunk in (0, 1):
        relay_channel(2, chunk)

    gg_out = jnp.zeros((C, C), FL)
    for chunk in (0, 1):
        all_a(2, chunk).wait_recv()
        for row in chunk_rows(chunk):
            prod = take_row(2, row)
            center = prod - jnp.mean(prod, axis=0, keepdims=True)
            inverse = lax.rsqrt(jnp.mean(center * center, axis=0, keepdims=True) + EPS)
            xh = center * inverse
            xn[row] = (xh * gain_out_c[:, :1]).astype(BF)
            lin = dot(w_out_t[...], xn[row])
            s = s_g[row]
            upd_t[row] = s * lin
            g = cot_t[row]
            d_lin[row] = (g * s).astype(BF)
            d_proj[row, 4 * C :, :] = (g * lin * s * (1.0 - s)).astype(BF)
            d_xn = dot(w_out_p[...], d_lin[row])
            both = d_xn * xh
            for tile in range(tiles):
                gg_out = gg_out + both[:, tile * C : (tile + 1) * C]
            h = d_xn * gain_out_c[:, :1]
            first = jnp.mean(h, axis=0, keepdims=True)
            second = jnp.mean(h * xh, axis=0, keepdims=True)
            place(3, row, inverse * (h - first - xh * second))
        send_rows(3, chunk)
    relay_rows(3, 0)
    relay_rows(3, 1)
    gw = jnp.zeros((C, C), FL)
    gw_gate = jnp.zeros((C, C), FL)
    for row in range(rows):
        gw = gw + dot(xn[row], d_lin[row], NT)
        gw_gate = gw_gate + dot(normed[row], d_proj[row, 4 * C :, :], NT)
    grads[4 * C : 5 * C, :] = gw_gate.astype(BF)
    grads[5 * C : 6 * C, :] = dot(perm[...], gw.astype(BF)).astype(BF)
    for row in range(rows):
        for tile in range(tiles):
            upd_ref[row, tile * C : (tile + 1) * C, :] = jnp.transpose(
                upd_t[row, :, tile * C : (tile + 1) * C]
            ).astype(BF)

    for chunk in (0, 1):
        take_channel(3, chunk, dprod_m)
        send_channel(4, chunk, dot(of(dprod_m, chunk), right_m[...]))
    turned_m[...] = dot(order_t[...], dprod_m[...], NT).astype(BF)
    for chunk in (0, 1):
        send_channel(5, chunk, dot(of(turned_m, chunk), left_m[...]))
    for stage in (4, 5):
        for chunk in (0, 1):
            relay_channel(stage, chunk)

    def write_rows(picked):
        for row in picked:
            zh = zhat[row]
            h = p_l[row] * gain_in_c[:, :1]
            first = jnp.mean(h, axis=0, keepdims=True)
            second = jnp.mean(h * zh, axis=0, keepdims=True)
            out = zinv[row] * (h - first - zh * second)
            for tile in range(tiles):
                gp_ref[row, tile * C : (tile + 1) * C, :] = jnp.transpose(
                    out[:, tile * C : (tile + 1) * C]
                ).astype(BF)

    gg_in = jnp.zeros((C, C), FL)
    for side, p_ref, s_ref in ((0, p_l, s_l), (1, p_r, s_r)):
        base = side * 2 * C
        total = jnp.zeros((C, 2 * C), FL)
        for chunk in (0, 1):
            all_a(4 + side, chunk).wait_recv()
            for row in chunk_rows(chunk):
                d = take_row(4 + side, row)
                s = s_ref[row]
                d_proj[row, base : base + C, :] = (d * s).astype(BF)
                d_proj[row, base + C : base + 2 * C, :] = (
                    d * p_ref[row] * s * (1.0 - s)
                ).astype(BF)
                total = total + dot(normed[row], d_proj[row, base : base + 2 * C, :], NT)
                if side == 1:
                    d_normed = dot(w_in_p[...], d_proj[row])
                    p_l[row] = d_normed
                    both = d_normed * zhat[row]
                    for tile in range(tiles):
                        gg_in = gg_in + both[:, tile * C : (tile + 1) * C]
            if side == 1 and chunk == 0:
                write_rows(chunk_rows(0))
        total = total.astype(BF)
        grads[base : base + C, :] = dot(total[:, :C], perm[...]).astype(BF)
        grads[base + C : base + 2 * C, :] = dot(total[:, C:], perm[...]).astype(BF)

    gg_in = jnp.sum(jnp.transpose(gg_in), axis=0, keepdims=True)
    gg_out = jnp.sum(jnp.transpose(gg_out), axis=0, keepdims=True)
    gg_out = dot(jnp.broadcast_to(gg_out, (GROWS, C)).astype(BF), perm[...])
    line = iota((GROWS, C), 0)
    grads[6 * C :, :] = jnp.where(line == 0, jnp.broadcast_to(gg_in, (GROWS, C)), gg_out).astype(BF)

    def both_ways(u, v):
        return v + core * (u - v), u + core * (v - u)

    for u in range(SIDE):
        for v in range(SIDE):
            at = (u * SIDE + v) * GROWS
            g_send[both_ways(u, v)] = grads[at : at + GROWS, :]

    in_a = a < SIDE
    in_b = b < SIDE
    owner = jnp.logical_and(in_a, in_b)
    for t in ROUND:
        at_a = (a + t) % LINE

        @pl.when(at_a < SIDE)
        def _():
            remote(
                g_send.at[at_a], g_recv.at[a], g_sems.at[0], g_sems.at[1], device(at_a, b, core)
            ).start()

    def some(ref, count, on_send, on_recv):
        return remote(ref.at[pl.ds(0, count)], ref.at[pl.ds(0, count)], on_send, on_recv, other)

    write_rows(range(2, 3))
    mine = b * 2 + core

    @pl.when(in_a)
    def _():
        g_recv[a] = g_send[a]
        some(g_recv, LINE - 1, g_sems.at[0], g_sems.at[1]).wait_recv()
        h_send[...] = jnp.sum(g_recv[...].astype(FL), axis=0).astype(BF)
        for t in (0,) + ROUND:
            at_b = (b + t) % LINE
            for turn in (0, 1):
                if t == 0 and turn == 0:
                    continue
                at_core = (core + turn) % 2

                @pl.when(at_b < SIDE)
                def _():
                    remote(
                        h_send.at[at_b],
                        h_recv.at[mine],
                        g_sems.at[2],
                        g_sems.at[3],
                        device(a, at_b, at_core),
                    ).start()

    write_rows(range(3, 4))

    @pl.when(owner)
    def _():
        h_recv[mine] = h_send[b]
        some(h_recv, GROUP - 1, g_sems.at[2], g_sems.at[3]).wait_recv()
        total = jnp.sum(h_recv[...].astype(FL), axis=0) * (1.0 / length)
        o_send[...] = total.astype(BF)
        for t in ROUND:
            remote(
                o_send, c_recv.at[b], g_sems.at[4], g_sems.at[5], device(a, (b + t) % LINE, core)
            ).start()
        c_recv[b] = o_send[...]

    write_rows(range(4, rows))

    @pl.when(in_a)
    def _():
        @pl.when(in_b)
        def _():
            some(c_recv, SIDE - 1, g_sems.at[4], g_sems.at[5]).wait_recv()

        @pl.when(jnp.logical_not(in_b))
        def _():
            some(c_recv, SIDE, g_sems.at[4], g_sems.at[5]).wait_recv()

        for t in ROUND:
            remote(
                c_recv, d_recv.at[a], g_sems.at[6], g_sems.at[7], device((a + t) % LINE, b, core)
            ).start()
        d_recv[a] = c_recv[...]
        some(d_recv, SIDE - 1, g_sems.at[6], g_sems.at[7]).wait_recv()

    @pl.when(jnp.logical_not(in_a))
    def _():
        some(d_recv, SIDE, g_sems.at[6], g_sems.at[7]).wait_recv()

    per = C // GROWS
    for u in range(SIDE):
        for v in range(SIDE):
            block, at = divmod(u * SIDE + v, per)
            value = d_recv[both_ways(u, v)].astype(FL)
            at = at * GROWS
            if block < 5:
                gwi_ref[at : at + GROWS, block * C : (block + 1) * C] = value
            elif block == 5:
                gwo_ref[at : at + GROWS, :] = value
            else:
                gains_ref[...] = value[:8]

    @pl.when(in_a)
    def _():
        some(g_send, SIDE - 1, g_sems.at[0], g_sems.at[1]).wait_send()
        some(g_recv, LINE - 1, g_sems.at[6], g_sems.at[7]).wait_send()

        @pl.when(in_b)
        def _():
            some(h_recv, GROUP - 3, g_sems.at[2], g_sems.at[3]).wait_send()
            some(h_recv, LINE - 1, g_sems.at[4], g_sems.at[5]).wait_send()

        @pl.when(jnp.logical_not(in_b))
        def _():
            some(h_recv, GROUP - 2, g_sems.at[2], g_sems.at[3]).wait_send()

    @pl.when(jnp.logical_not(in_a))
    def _():
        some(g_send, SIDE, g_sems.at[0], g_sems.at[1]).wait_send()

    for stage in range(6):
        for chunk in (0, 1):
            all_a(stage, chunk).wait_send()
            all_b(stage, chunk).wait_send()


def on_device(pair_input, gain_in, w_in, w_out, product_gain, cotangent):
    rows, length, width = pair_input.shape
    piece = sum(padded(count, length // C) for _, count in CHUNKS)
    held = (rows, C, length)
    square = (length, length)
    vmem = pl.BlockSpec(memory_space=pltpu.VMEM)
    sem = pltpu.SemaphoreType.DMA
    upd, gp, gwi, gwo, gains = pl.pallas_call(
        functools.partial(kernel, rows, length),
        out_shape=(
            jax.ShapeDtypeStruct(pair_input.shape, BF),
            jax.ShapeDtypeStruct(pair_input.shape, BF),
            jax.ShapeDtypeStruct(w_in.shape, FL),
            jax.ShapeDtypeStruct(w_out.shape, FL),
            jax.ShapeDtypeStruct((8, C), FL),
        ),
        in_specs=[vmem] * 6,
        out_specs=[vmem] * 5,
        scratch_shapes=[
            pltpu.VMEM((6, LINE, rows, GROUP, length), BF),
            pltpu.VMEM((6, LINE, rows, GROUP, length), BF),
            pltpu.VMEM((6, GROUP, piece, C), BF),
            pltpu.VMEM((6, GROUP, piece, C), BF),
            pltpu.VMEM((GROUP * (piece + 1), C), FL),
            pltpu.VMEM((SIDE, SIDE, GROWS, C), BF),
            pltpu.VMEM((LINE, SIDE, GROWS, C), BF),
            pltpu.VMEM((SIDE, GROWS, C), BF),
            pltpu.VMEM((GROUP, GROWS, C), BF),
            pltpu.VMEM((GROWS, C), BF),
            pltpu.VMEM((SIDE, GROWS, C), BF),
            pltpu.VMEM((SIDE, SIDE, GROWS, C), BF),
            *[pltpu.VMEM(square, BF)] * 6,
            pltpu.VMEM((LINE * GROUP * CHUNKS[1][1], length), FL),
            pltpu.VMEM(held, FL),
            pltpu.VMEM((rows, 1, length), FL),
            pltpu.VMEM(held, BF),
            *[pltpu.VMEM(held, FL)] * 7,
            pltpu.VMEM(held, BF),
            pltpu.VMEM(held, BF),
            pltpu.VMEM((rows, 5 * C, length), BF),
            pltpu.VMEM((5 * C, C), BF),
            pltpu.VMEM((C, 5 * C), BF),
            pltpu.VMEM((C, C), BF),
            pltpu.VMEM((C, C), BF),
            pltpu.VMEM((C, C), FL),
            pltpu.VMEM((C, C), FL),
            pltpu.VMEM((C, C), BF),
            pltpu.VMEM((SIDE * SIDE * GROWS, C), BF),
            sem((6, 2)),
            sem((6, 2)),
            sem((6, 2)),
            sem((6, 2)),
            sem((8,)),
        ],
        compiler_params=pltpu.CompilerParams(
            collective_id=0, has_side_effects=True, vmem_limit_bytes=58 * 2**20
        ),
    )(pair_input, gain_in.reshape(1, C), w_in, w_out, product_gain.reshape(1, C), cotangent)
    return upd, gp, gwi, gwo, gains[0], gains[1]


def solution(mesh):
    return jax.shard_map(
        on_device,
        mesh=mesh,
        in_specs=(
            P(("crop", "res"), None, None),
            P(),
            P(),
            P(),
            P(),
            P(("crop", "res"), None, None),
        ),
        out_specs=(
            P(("crop", "res"), None, None),
            P(("crop", "res"), None, None),
            P("crop", None),
            P("crop", None),
            P("crop"),
            P("crop"),
        ),
        check_vma=False,
    )
```

time: 759 us -> 180 us (0.24)
  blocking collectives: 322 us -> 0 us
  waiting for transfers between devices: 280 us -> 0 us
  Pallas kernels: 0 us -> 172 us
  starting transfers between devices: 39.6 us -> 0 us
  local copies, waits for them, and re-layouts: 44.9 us -> 6.09 us
  other arithmetic: 27.1 us -> 0 us
  matrix products: 23.1 us -> 0 us
  between operations: 14.6 us -> 0.65 us
    psum x1 -> x0, blocking collectives: 246 us -> none  [on_device(): lax.psum((gw_in, gw_out, gg_in, product_gain_gradient), 'res')]
    psum x1 -> x0, waiting for transfers between devices: 185 us -> none  [on_device(): lax.psum((gw_in, gw_out, gg_in, product_gain_gradient), 'res')]
    pallas_call x0 -> x1, Pallas kernels: none -> 172 us  [on_device(): pl.pallas_call(functools.partial(kernel, rows, length), out_shape=(jax.Sh...]
    all_to_all x4 -> x0, waiting for transfers between devices: 95.7 us -> none  [the longest x1 34.5 us: on_device(): lax.all_to_all(left_rows, 'res', split_axis=1, concat_axis=0, tiled=True)]
    all_to_all x2 -> x0, blocking collectives: 75.8 us -> none  [the longest x1 42 us: on_device(): lax.all_to_all(product_gradient, 'res', split_axis=1, concat_axis=0, tile...]
    all_to_all x4 -> x0, starting transfers between devices: 39.6 us -> none  [the longest x1 18.4 us: on_device(): lax.all_to_all(left_rows, 'res', split_axis=1, concat_axis=0, tiled=True)]
    unnamed x45 -> x10, local copies, waits for them, and re-layouts: 31.6 us -> 4.82 us
    dot_general x12 -> x0, matrix products: 23.1 us -> none  [the longest x1 3.35 us: on_device(): jnp.einsum('icj,ick->jck', d_prod_cols, left_cols, preferred_element_type...]
  transfers between devices with their start and end apart: 5 -> 0, of which waited for: 5 -> 0; matrix products, arithmetic and copies ran while one was open for 4% -> 0% of each run, Pallas kernels for 0% -> 0%
where the time goes in v2:
time: 180 us; the launch traced here: 179 us
  Pallas kernels  172 us (96%)
  local copies, waits for them, and re-layouts  6.09 us (3%)
    pallas_call x1, Pallas kernels, on_device(): pl.pallas_call(functools.partial(kernel, rows, length), out_shape=(jax.Sh...  172 us
    unnamed x10, local copies, waits for them, and re-layouts  4.82 us

profile of v2, /device:TPU:1, one launch (start us, length us, event | category | flops | bytes accessed | tf_op | source)
XLA Modules:
  0.0 178.9 jit_solution(7455170425691065248)
XLA Ops:
  0.6 172.2 %shard_map.109 = (bf16[5,640,128]{2,1,0:T(8,128)(2,1)}, bf16[5,640,128]{2,1,0:T(8,128)(2,1)}, f32[128,640]{1,0:T(8,128)}, f32[128,128]{1,0:T(8,128)}, f32[8,128]{1,0:T(8,128)}) custom-call(bf16[5,640,128]{2,1,0:T(8,128)(2,1)} %z_ref.1, f32[1,128]{1,0:T(1,128)} %bitcast.6, bf16[128,640]{1,0:T(8,128)(2,1)} %w_in_ref.1, bf16[128,128]{1,0:T(8,128)(2,1)} %w_out_ref.1, ...), custom_call_target="tpu_custom_call" | custom-call | tf_op jit(solution)/shard_map/pallas_call | solution.py:548
  172.8 1.3 slice_bitcast_fusion
  174.1 0.0 copy-start
  174.1 2.2 %copy.16 = bf16[5,640,128]{2,1,0:T(8,128)(2,1)} copy(bf16[5,640,128]{2,1,0:T(8,128)(2,1)} %get-tuple-element.24) | data formatting | bytes 1638400
  176.2 0.0 copy-done
  176.2 0.0 copy-start.1
  176.2 0.9 copy.17
  177.1 0.3 copy-done.1
  177.4 0.0 copy-start.2
  177.4 0.7 copy.18
  178.1 0.1 copy-done.2
  178.3 0.6 copy.19
Async XLA Ops:
  174.1 2.2 %copy-start = (bf16[5,640,128]{2,1,0:T(8,128)(2,1)S(1)}, bf16[5,640,128]{2,1,0:T(8,128)(2,1)}, u32[]{:S(2)}) copy-start(bf16[5,640,128]{2,1,0:T(8,128)(2,1)} %get-tuple-element.25) | copy-start | bytes 2457604
  176.2 1.2 copy-start.1
  177.4 0.9 copy-start.2

commit v3 on v2

--- a/solution.py
+++ b/solution.py
@@ -16,7 +16,8 @@
 GROWS = 16
 SIDE = 7
 ROUND = (1, 7, 2, 6, 3, 5, 4)
-CHUNKS = ((0, 2), (2, 3))
+CHUNKS = ((0, 1), (1, 2), (3, 2))
+ALL = range(len(CHUNKS))
 
 
 def dot(a, b, dims=((1,), (0,))):
@@ -37,21 +38,20 @@
 def kernel(
     rows, length,
     z_ref, gain_in_ref, w_in_ref, w_out_ref, gain_out_ref, cot_ref,
-    upd_ref, gp_ref, gwi_ref, gwo_ref, gains_ref,
-    send1, recv1, send2, recv2, mixed,
+    upd_ref, gp_ref, gwi_ref, gwo_ref, ggi_ref, ggo_ref,
+    send1, recv1, send2, recv2, send_w, recv_w, mixed, swap, upd_v, gp_v,
     g_send, g_recv, h_send, h_recv, o_send, c_recv, d_recv,
     left_m, right_m, dprod_m, turned_m, order, order_t, wide,
     zhat, zinv, normed, p_l, s_l, p_r, s_r, s_g, cot_t, upd_t, xn, d_lin, d_proj,
     w_in_t, w_in_p, w_out_t, w_out_p, gain_in_c, gain_out_c, perm, grads,
-    send_sem1, recv_sem1, send_sem2, recv_sem2, g_sems,
+    send_sem1, recv_sem1, send_sem2, recv_sem2, g_sems, out_sems,
 ):
     tiles = length // C
 
     def sizes(chunk):
         first, count = CHUNKS[chunk]
-        start = 0 if chunk == 0 else padded(CHUNKS[0][1], tiles)
-        base = 0 if chunk == 0 else LINE * GROUP * CHUNKS[0][1]
-        return first, count, start, padded(count, tiles), LINE * count, base
+        base = LINE * GROUP * first
+        return first, count, padded(count, tiles), LINE * count, base
 
     me = lax.axis_index("res")
     z = me // GROUP
@@ -114,35 +114,44 @@
         )
 
     def all_b(stage, chunk):
-        _, _, start, piece, _, _ = sizes(chunk)
+        out, into = pieces(stage, chunk)
         return remote(
-            send2.at[stage, pl.ds(0, GROUP - 1), pl.ds(start, piece)],
-            recv2.at[stage, pl.ds(0, GROUP - 1), pl.ds(start, piece)],
+            out.at[pl.ds(0, GROUP - 1)],
+            into.at[pl.ds(0, GROUP - 1)],
             send_sem2.at[stage, chunk],
             recv_sem2.at[stage, chunk],
             other,
         )
 
+    def pieces(stage, chunk):
+        if CHUNKS[chunk][1] == 1:
+            return send2.at[stage], recv2.at[stage]
+        return send_w.at[stage, chunk - 1], recv_w.at[stage, chunk - 1]
+
+    def swapped(value):
+        return dot(swap[...], value.reshape(GROUP * GROUP, length)).astype(BF)
+
     def place(stage, row, value):
         value = value.astype(BF)
         for at in range(LINE):
             send1[stage, at, row] = value[at * GROUP : (at + 1) * GROUP]
 
     def relay_rows(stage, chunk):
-        first, count, start, piece, _, _ = sizes(chunk)
-        part = pl.ds(start, piece)
+        first, count, piece, _, _ = sizes(chunk)
+        out, into = pieces(stage, chunk)
         stride = piece + 1
         all_a(stage, chunk).wait_recv()
-        for at in range(LINE):
-            for row in range(count):
-                block = recv1[stage, at, first + row].astype(FL)
+        if count == 2:
+            out[...] = swapped(recv1[stage, :, first : first + 2]).reshape(GROUP, GROUP, length)
+        else:
+            for at in range(LINE):
+                block = recv1[stage, at, first].astype(FL)
                 for tile in range(tiles):
-                    where = (at * count + row) * tiles + tile
-                    mixed[pl.ds(where, GROUP, stride=stride), :] = block[
+                    mixed[pl.ds(at * tiles + tile, GROUP, stride=stride), :] = block[
                         :, tile * C : (tile + 1) * C
                     ]
-        for q in range(GROUP):
-            send2[stage, q, part] = mixed[q * stride : q * stride + piece, :].astype(BF)
+            for q in range(GROUP):
+                out[q] = mixed[q * stride : q * stride + piece, :].astype(BF)
         mine = b * 2 + core
         for t in (0,) + ROUND:
             at_b = (b + t) % LINE
@@ -151,21 +160,24 @@
                     continue
                 at_core = (core + turn) % 2
                 remote(
-                    send2.at[stage, at_b * 2 + at_core, part],
-                    recv2.at[stage, mine, part],
+                    out.at[at_b * 2 + at_core],
+                    into.at[mine],
                     send_sem2.at[stage, chunk],
                     recv_sem2.at[stage, chunk],
                     device(a, at_b, at_core),
                 ).start()
-        recv2[stage, mine, part] = send2[stage, mine, part]
+        into[mine] = out[mine]
 
     def take_channel(stage, chunk, into):
-        first, count, start, piece, lot, base = sizes(chunk)
+        first, count, piece, lot, base = sizes(chunk)
         all_b(stage, chunk).wait_recv()
+        if count == 2:
+            into[base : base + GROUP * lot, :] = pieces(stage, chunk)[1][...].reshape(
+                GROUP * lot, length
+            )
+            return
         for slot in range(GROUP):
-            mixed[slot * piece : (slot + 1) * piece, :] = recv2[
-                stage, slot, start : start + piece
-            ].astype(FL)
+            mixed[slot * piece : (slot + 1) * piece, :] = recv2[stage, slot].astype(FL)
         for at in range(LINE):
             top = base + at * 2 * lot
             for tile in range(tiles):
@@ -178,27 +190,33 @@
                 )
 
     def of(factor, chunk):
-        _, _, _, _, lot, base = sizes(chunk)
+        _, _, _, lot, base = sizes(chunk)
         return factor[base : base + GROUP * lot, :]
 
     def send_channel(stage, chunk, whole):
-        _, _, start, piece, lot, _ = sizes(chunk)
-        slab = pl.ds(start, piece)
-        wide[: GROUP * lot, :] = whole
+        _, _, piece, lot, _ = sizes(chunk)
+        out, into = pieces(stage, chunk)
+        single = CHUNKS[chunk][1] == 1
+        if single:
+            wide[...] = whole
+        else:
+            out[...] = whole.astype(BF).reshape(GROUP, GROUP, length)
         for t in (0,) + ROUND:
             at_b = (b + t) % LINE
-            part = wide[pl.ds(pl.multiple_of(at_b * 2 * lot, GROUP), 2 * lot), :]
+            if single:
+                part = wide[pl.ds(pl.multiple_of(at_b * 2 * lot, GROUP), 2 * lot), :]
+                for k in (0, 1):
+                    for tile in range(tiles):
+                        mixed[pl.ds(k * piece + tile, lot, stride=tiles), :] = part[
+                            k * lot : (k + 1) * lot, tile * C : (tile + 1) * C
+                        ]
             for k in (0, 1):
-                for tile in range(tiles):
-                    mixed[pl.ds(k * piece + tile, lot, stride=tiles), :] = part[
-                        k * lot : (k + 1) * lot, tile * C : (tile + 1) * C
-                    ]
-            for k in (0, 1):
-                send2[stage, at_b * 2 + k, slab] = mixed[k * piece : (k + 1) * piece, :].astype(BF)
+                if single:
+                    out[at_b * 2 + k] = mixed[k * piece : (k + 1) * piece, :].astype(BF)
                 to = (at_b * GROUP + y * 2) if k == 0 else (z * GROUP + at_b * 2 + 1)
                 copy = remote(
-                    send2.at[stage, at_b * 2 + k, slab],
-                    recv2.at[stage, (z if k == 0 else y) * 2 + core, slab],
+                    out.at[at_b * 2 + k],
+                    into.at[(z if k == 0 else y) * 2 + core],
                     send_sem2.at[stage, chunk],
                     recv_sem2.at[stage, chunk],
                     to,
@@ -207,7 +225,7 @@
 
                     @pl.when(core == k)
                     def _():
-                        recv2[stage, at_b * 2 + k, slab] = send2[stage, at_b * 2 + k, slab]
+                        into[at_b * 2 + k] = out[at_b * 2 + k]
 
                     @pl.when(core != k)
                     def _():
@@ -217,19 +235,19 @@
                     copy.start()
 
     def relay_channel(stage, chunk):
-        first, count, start, piece, _, _ = sizes(chunk)
+        first, count, piece, _, _ = sizes(chunk)
         stride = piece + 1
         all_b(stage, chunk).wait_recv()
-        for q in range(GROUP):
-            mixed[q * stride : q * stride + piece, :] = recv2[
-                stage, q, start : start + piece
-            ].astype(FL)
-        for at in range(LINE):
-            for row in range(count):
+        into = pieces(stage, chunk)[1]
+        if count == 2:
+            send1[stage, :, first : first + 2] = swapped(into[...]).reshape(LINE, 2, GROUP, length)
+        else:
+            for q in range(GROUP):
+                mixed[q * stride : q * stride + piece, :] = into[q].astype(FL)
+            for at in range(LINE):
                 for tile in range(tiles):
-                    where = (at * count + row) * tiles + tile
-                    send1[stage, at, first + row, :, tile * C : (tile + 1) * C] = mixed[
-                        pl.ds(where, GROUP, stride=stride), :
+                    send1[stage, at, first, :, tile * C : (tile + 1) * C] = mixed[
+                        pl.ds(at * tiles + tile, GROUP, stride=stride), :
                     ].astype(BF)
         send_rows(stage, chunk)
 
@@ -248,20 +266,17 @@
     home = (q >> 4) * step_a + ((q >> 1) & 7) * step_b + (q & 1)
     perm_f = (home == iota((C, C), 1)).astype(FL)
     perm[...] = perm_f.astype(BF)
-    for block in range(5):
+    def weights(block):
         sort = perm[...] if block < 4 else eye
         cols = slice(block * C, (block + 1) * C)
         w_in_t[cols, :] = dot(sort, w_in_ref[:, cols], NT).astype(BF)
         w_in_p[:, cols] = dot(w_in_ref[:, cols], sort, NT).astype(BF)
-    w_out_p[...] = dot(perm[...], w_out_ref[...]).astype(BF)
-    w_out_t[...] = jnp.transpose(dot(perm[...], w_out_ref[...])).astype(BF)
+
+    weights(2)
+    weights(3)
     gain_in_c[...] = jnp.transpose(jnp.broadcast_to(gain_in_ref[...], (C, C)))
-    gain_out_c[...] = jnp.broadcast_to(
-        jnp.sum(perm_f * gain_out_ref[...], axis=1, keepdims=True), (C, C)
-    )
-    mixed[...] = jnp.zeros(mixed.shape, FL)
-
-    for chunk in (0, 1):
+
+    for chunk in ALL:
         for row in chunk_rows(chunk):
             zt = dot(eye, z_ref[row], NT)
             center = zt - jnp.mean(zt, axis=0, keepdims=True)
@@ -270,40 +285,47 @@
             zhat[row] = zh
             zinv[row] = inverse
             normed[row] = (zh * gain_in_c[:, :1]).astype(BF)
+            proj = dot(w_in_t[2 * C : 4 * C, :], normed[row])
+            s_r[row] = sigmoid(proj[C:])
+            p_r[row] = proj[:C]
+            place(1, row, p_r[row] * s_r[row])
+        if chunk == 0:
+            pl.semaphore_wait(barrier, 4 * LINE - 3)
+        send_rows(1, chunk)
+    for block in (0, 1, 4):
+        weights(block)
+    for chunk in ALL:
+        for row in chunk_rows(chunk):
             proj = dot(w_in_t[: 2 * C, :], normed[row])
             s_l[row] = sigmoid(proj[C:])
             p_l[row] = proj[:C]
             place(0, row, p_l[row] * s_l[row])
-        if chunk == 0:
-            pl.semaphore_wait(barrier, 4 * LINE - 3)
         send_rows(0, chunk)
-    for chunk in (0, 1):
-        for row in chunk_rows(chunk):
-            proj = dot(w_in_t[2 * C : 4 * C, :], normed[row])
-            s_r[row] = sigmoid(proj[C:])
-            p_r[row] = proj[:C]
-            place(1, row, p_r[row] * s_r[row])
-        send_rows(1, chunk)
-    relay_rows(0, 0)
-    relay_rows(0, 1)
-    for row in range(rows):
-        s_g[row] = sigmoid(dot(w_in_t[4 * C :, :], normed[row]))
-    relay_rows(1, 0)
-    relay_rows(1, 1)
-    for row in range(rows):
-        cot_t[row] = dot(eye, cot_ref[row], NT)
+
+    w_out_p[...] = dot(perm[...], w_out_ref[...]).astype(BF)
+    w_out_t[...] = jnp.transpose(dot(perm[...], w_out_ref[...])).astype(BF)
+    gain_out_c[...] = jnp.broadcast_to(
+        jnp.sum(perm_f * gain_out_ref[...], axis=1, keepdims=True), (C, C)
+    )
+    mixed[...] = jnp.zeros(mixed.shape, FL)
+    p = iota((1, GROUP * GROUP), 1)
+    turned = (p & (GROUP - 1)) * GROUP + (p >> 4)
+    swap[...] = (iota((GROUP * GROUP, GROUP * GROUP), 0) == turned).astype(FL).astype(BF)
 
     def natural(p):
-        split = LINE * GROUP * CHUNKS[0][1]
-        second = p >= split
-        count = jnp.where(second, float(CHUNKS[1][1]), float(CHUNKS[0][1]))
-        pf = p.astype(FL) + 0.5 - jnp.where(second, float(split), 0.0)
+        count = jnp.full(p.shape, float(CHUNKS[0][1]), FL)
+        first = jnp.zeros(p.shape, FL)
+        for start, size in CHUNKS[1:]:
+            later = p >= LINE * GROUP * start
+            count = jnp.where(later, float(size), count)
+            first = jnp.where(later, float(start), first)
+        pf = p.astype(FL) + 0.5 - first * (LINE * GROUP)
         at_b = jnp.floor(pf / (count * GROUP))
         pf = pf - at_b * (count * GROUP)
         at_core = jnp.floor(pf / (count * LINE))
         pf = pf - at_core * (count * LINE)
         at_a = jnp.floor(pf / count)
-        row = pf - 0.5 - at_a * count + jnp.where(second, float(CHUNKS[1][0]), 0.0)
+        row = pf - 0.5 - at_a * count + first
         at_z = at_b + at_core * (at_a - at_b)
         at_y = at_a + at_core * (at_b - at_a)
         return ((at_z * GROUP + at_y * 2 + at_core) * rows + row + 0.5).astype(jnp.int32)
@@ -313,19 +335,26 @@
         (iota((length, length), 1) == natural(iota((length, 1), 0))).astype(FL).astype(BF)
     )
 
-    take_channel(0, 0, left_m)
-    take_channel(0, 1, left_m)
-    take_channel(1, 0, turned_m)
-    take_channel(1, 1, turned_m)
+    for chunk in ALL:
+        relay_rows(1, chunk)
+    for row in range(rows):
+        s_g[row] = sigmoid(dot(w_in_t[4 * C :, :], normed[row]))
+    for chunk in ALL:
+        relay_rows(0, chunk)
+    for row in range(rows):
+        cot_t[row] = dot(eye, cot_ref[row], NT)
+    for chunk in ALL:
+        take_channel(1, chunk, turned_m)
     right_m[...] = dot(order[...], turned_m[...]).astype(BF)
-    for chunk in (0, 1):
+    for chunk in ALL:
+        take_channel(0, chunk, left_m)
         send_channel(2, chunk, dot(of(left_m, chunk), right_m[...], NT))
-    for chunk in (0, 1):
-        relay_channel(2, chunk)
-
-    gg_out = jnp.zeros((C, C), FL)
-    for chunk in (0, 1):
+
+    gg_parts = []
+
+    def middle(chunk):
         all_a(2, chunk).wait_recv()
+        gg_out = jnp.zeros((C, C), FL)
         for row in chunk_rows(chunk):
             prod = take_row(2, row)
             center = prod - jnp.mean(prod, axis=0, keepdims=True)
@@ -347,8 +376,35 @@
             second = jnp.mean(h * xh, axis=0, keepdims=True)
             place(3, row, inverse * (h - first - xh * second))
         send_rows(3, chunk)
+        gg_parts.append(gg_out)
+
+    def left_back(chunk):
+        take_channel(3, chunk, dprod_m)
+        send_channel(4, chunk, dot(of(dprod_m, chunk), right_m[...]))
+
+    def right_back(chunk):
+        send_channel(5, chunk, dot(of(turned_m, chunk), left_m[...]))
+
+    relay_channel(2, 0)
+    relay_channel(2, 1)
+    middle(0)
+    relay_channel(2, 2)
+    middle(1)
     relay_rows(3, 0)
+    middle(2)
     relay_rows(3, 1)
+    left_back(0)
+    relay_rows(3, 2)
+    left_back(1)
+    left_back(2)
+    relay_channel(4, 0)
+    turned_m[...] = dot(order_t[...], dprod_m[...], NT).astype(BF)
+    right_back(0)
+    relay_channel(4, 1)
+    right_back(1)
+    relay_channel(4, 2)
+    right_back(2)
+    gg_out = gg_parts[0] + gg_parts[1] + gg_parts[2]
     gw = jnp.zeros((C, C), FL)
     gw_gate = jnp.zeros((C, C), FL)
     for row in range(rows):
@@ -356,21 +412,17 @@
         gw_gate = gw_gate + dot(normed[row], d_proj[row, 4 * C :, :], NT)
     grads[4 * C : 5 * C, :] = gw_gate.astype(BF)
     grads[5 * C : 6 * C, :] = dot(perm[...], gw.astype(BF)).astype(BF)
-    for row in range(rows):
-        for tile in range(tiles):
-            upd_ref[row, tile * C : (tile + 1) * C, :] = jnp.transpose(
-                upd_t[row, :, tile * C : (tile + 1) * C]
-            ).astype(BF)
-
-    for chunk in (0, 1):
-        take_channel(3, chunk, dprod_m)
-        send_channel(4, chunk, dot(of(dprod_m, chunk), right_m[...]))
-    turned_m[...] = dot(order_t[...], dprod_m[...], NT).astype(BF)
-    for chunk in (0, 1):
-        send_channel(5, chunk, dot(of(turned_m, chunk), left_m[...]))
-    for stage in (4, 5):
-        for chunk in (0, 1):
-            relay_channel(stage, chunk)
+
+    def leave(held, out, which, row):
+        return pltpu.make_async_copy(held.at[row], out.at[row], out_sems.at[which, row])
+
+    def write_update(picked):
+        for row in picked:
+            for tile in range(tiles):
+                upd_v[row, tile * C : (tile + 1) * C, :] = jnp.transpose(
+                    upd_t[row, :, tile * C : (tile + 1) * C]
+                ).astype(BF)
+            leave(upd_v, upd_ref, 0, row).start()
 
     def write_rows(picked):
         for row in picked:
@@ -380,35 +432,52 @@
             second = jnp.mean(h * zh, axis=0, keepdims=True)
             out = zinv[row] * (h - first - zh * second)
             for tile in range(tiles):
-                gp_ref[row, tile * C : (tile + 1) * C, :] = jnp.transpose(
+                gp_v[row, tile * C : (tile + 1) * C, :] = jnp.transpose(
                     out[:, tile * C : (tile + 1) * C]
                 ).astype(BF)
-
-    gg_in = jnp.zeros((C, C), FL)
-    for side, p_ref, s_ref in ((0, p_l, s_l), (1, p_r, s_r)):
+            leave(gp_v, gp_ref, 1, row).start()
+
+    def factor_back(side, chunk, total):
+        p_ref, s_ref = ((p_l, s_l), (p_r, s_r))[side]
         base = side * 2 * C
-        total = jnp.zeros((C, 2 * C), FL)
-        for chunk in (0, 1):
-            all_a(4 + side, chunk).wait_recv()
-            for row in chunk_rows(chunk):
-                d = take_row(4 + side, row)
-                s = s_ref[row]
-                d_proj[row, base : base + C, :] = (d * s).astype(BF)
-                d_proj[row, base + C : base + 2 * C, :] = (
-                    d * p_ref[row] * s * (1.0 - s)
-                ).astype(BF)
-                total = total + dot(normed[row], d_proj[row, base : base + 2 * C, :], NT)
-                if side == 1:
-                    d_normed = dot(w_in_p[...], d_proj[row])
-                    p_l[row] = d_normed
-                    both = d_normed * zhat[row]
-                    for tile in range(tiles):
-                        gg_in = gg_in + both[:, tile * C : (tile + 1) * C]
-            if side == 1 and chunk == 0:
-                write_rows(chunk_rows(0))
+        all_a(4 + side, chunk).wait_recv()
+        for row in chunk_rows(chunk):
+            d = take_row(4 + side, row)
+            s = s_ref[row]
+            d_proj[row, base : base + C, :] = (d * s).astype(BF)
+            d_proj[row, base + C : base + 2 * C, :] = (d * p_ref[row] * s * (1.0 - s)).astype(BF)
+            total = total + dot(normed[row], d_proj[row, base : base + 2 * C, :], NT)
+        return total
+
+    def weights_back(side, total):
+        base = side * 2 * C
         total = total.astype(BF)
         grads[base : base + C, :] = dot(total[:, :C], perm[...]).astype(BF)
         grads[base + C : base + 2 * C, :] = dot(total[:, C:], perm[...]).astype(BF)
+
+    total = jnp.zeros((C, 2 * C), FL)
+    write_update(range(0, 2))
+    total = factor_back(0, 0, total)
+    relay_channel(5, 0)
+    total = factor_back(0, 1, total)
+    relay_channel(5, 1)
+    write_update(range(2, rows))
+    total = factor_back(0, 2, total)
+    weights_back(0, total)
+    relay_channel(5, 2)
+    total = jnp.zeros((C, 2 * C), FL)
+    gg_in = jnp.zeros((C, C), FL)
+    for chunk in ALL:
+        total = factor_back(1, chunk, total)
+        for row in chunk_rows(chunk):
+            d_normed = dot(w_in_p[...], d_proj[row])
+            p_l[row] = d_normed
+            both = d_normed * zhat[row]
+            for tile in range(tiles):
+                gg_in = gg_in + both[:, tile * C : (tile + 1) * C]
+        if chunk < 2:
+            write_rows(chunk_rows(chunk))
+    weights_back(1, total)
 
     gg_in = jnp.sum(jnp.transpose(gg_in), axis=0, keepdims=True)
     gg_out = jnp.sum(jnp.transpose(gg_out), axis=0, keepdims=True)
@@ -439,7 +508,6 @@
     def some(ref, count, on_send, on_recv):
         return remote(ref.at[pl.ds(0, count)], ref.at[pl.ds(0, count)], on_send, on_recv, other)
 
-    write_rows(range(2, 3))
     mine = b * 2 + core
 
     @pl.when(in_a)
@@ -512,7 +580,8 @@
             elif block == 5:
                 gwo_ref[at : at + GROWS, :] = value
             else:
-                gains_ref[...] = value[:8]
+                ggi_ref[...] = value[0:1]
+                ggo_ref[...] = value[1:2]
 
     @pl.when(in_a)
     def _():
@@ -533,35 +602,66 @@
         some(g_send, SIDE, g_sems.at[0], g_sems.at[1]).wait_send()
 
     for stage in range(6):
-        for chunk in (0, 1):
+        for chunk in ALL:
             all_a(stage, chunk).wait_send()
             all_b(stage, chunk).wait_send()
+    for row in range(rows):
+        leave(upd_v, upd_ref, 0, row).wait()
+        leave(gp_v, gp_ref, 1, row).wait()
+
+
+def write(rows, *refs):
+    into, out = refs[-2:]
+    pairs = []
+    for src, held, dst in zip(refs[:6], refs[12:18], refs[6:12]):
+        if len(src.shape) == 3:
+            pairs += [(src.at[row], held.at[row], dst.at[row]) for row in range(rows)]
+        else:
+            pairs.append((src, held, dst))
+    reads = [pltpu.make_async_copy(s, h, into.at[i]) for i, (s, h, _) in enumerate(pairs)]
+    writes = [pltpu.make_async_copy(h, d, out.at[i]) for i, (_, h, d) in enumerate(pairs)]
+    for copy in reads:
+        copy.start()
+    for read, copy in zip(reads, writes):
+        read.wait()
+        copy.start()
+    for copy in writes:
+        copy.wait()
 
 
 def on_device(pair_input, gain_in, w_in, w_out, product_gain, cotangent):
     rows, length, width = pair_input.shape
-    piece = sum(padded(count, length // C) for _, count in CHUNKS)
+    piece = padded(1, length // C)
+    pairs = len(CHUNKS) - 1
+    anywhere = pl.BlockSpec(memory_space=pl.ANY)
     held = (rows, C, length)
     square = (length, length)
     vmem = pl.BlockSpec(memory_space=pltpu.VMEM)
     sem = pltpu.SemaphoreType.DMA
-    upd, gp, gwi, gwo, gains = pl.pallas_call(
+    shapes = (
+        jax.ShapeDtypeStruct(pair_input.shape, BF),
+        jax.ShapeDtypeStruct(pair_input.shape, BF),
+        jax.ShapeDtypeStruct(w_in.shape, FL),
+        jax.ShapeDtypeStruct(w_out.shape, FL),
+        jax.ShapeDtypeStruct((1, C), FL),
+        jax.ShapeDtypeStruct((1, C), FL),
+    )
+    results = pl.pallas_call(
         functools.partial(kernel, rows, length),
-        out_shape=(
-            jax.ShapeDtypeStruct(pair_input.shape, BF),
-            jax.ShapeDtypeStruct(pair_input.shape, BF),
-            jax.ShapeDtypeStruct(w_in.shape, FL),
-            jax.ShapeDtypeStruct(w_out.shape, FL),
-            jax.ShapeDtypeStruct((8, C), FL),
-        ),
+        out_shape=shapes,
         in_specs=[vmem] * 6,
-        out_specs=[vmem] * 5,
+        out_specs=[anywhere] * 2 + [vmem] * 4,
         scratch_shapes=[
             pltpu.VMEM((6, LINE, rows, GROUP, length), BF),
             pltpu.VMEM((6, LINE, rows, GROUP, length), BF),
             pltpu.VMEM((6, GROUP, piece, C), BF),
             pltpu.VMEM((6, GROUP, piece, C), BF),
+            pltpu.VMEM((6, pairs, GROUP, GROUP, length), BF),
+            pltpu.VMEM((6, pairs, GROUP, GROUP, length), BF),
             pltpu.VMEM((GROUP * (piece + 1), C), FL),
+            pltpu.VMEM((GROUP * GROUP, GROUP * GROUP), BF),
+            pltpu.VMEM(pair_input.shape, BF),
+            pltpu.VMEM(pair_input.shape, BF),
             pltpu.VMEM((SIDE, SIDE, GROWS, C), BF),
             pltpu.VMEM((LINE, SIDE, GROWS, C), BF),
             pltpu.VMEM((SIDE, GROWS, C), BF),
@@ -570,7 +670,7 @@
             pltpu.VMEM((SIDE, GROWS, C), BF),
             pltpu.VMEM((SIDE, SIDE, GROWS, C), BF),
             *[pltpu.VMEM(square, BF)] * 6,
-            pltpu.VMEM((LINE * GROUP * CHUNKS[1][1], length), FL),
+            pltpu.VMEM((LINE * GROUP, length), FL),
             pltpu.VMEM(held, FL),
             pltpu.VMEM((rows, 1, length), FL),
             pltpu.VMEM(held, BF),
@@ -586,17 +686,27 @@
             pltpu.VMEM((C, C), FL),
             pltpu.VMEM((C, C), BF),
             pltpu.VMEM((SIDE * SIDE * GROWS, C), BF),
-            sem((6, 2)),
-            sem((6, 2)),
-            sem((6, 2)),
-            sem((6, 2)),
+            sem((6, len(CHUNKS))),
+            sem((6, len(CHUNKS))),
+            sem((6, len(CHUNKS))),
+            sem((6, len(CHUNKS))),
             sem((8,)),
+            sem((2, rows)),
         ],
         compiler_params=pltpu.CompilerParams(
             collective_id=0, has_side_effects=True, vmem_limit_bytes=58 * 2**20
         ),
     )(pair_input, gain_in.reshape(1, C), w_in, w_out, product_gain.reshape(1, C), cotangent)
-    return upd, gp, gwi, gwo, gains[0], gains[1]
+    upd, gp, gwi, gwo, ggi, ggo = pl.pallas_call(
+        functools.partial(write, rows),
+        out_shape=shapes,
+        in_specs=[anywhere] * 6,
+        out_specs=[anywhere] * 6,
+        scratch_shapes=[pltpu.VMEM(shape.shape, shape.dtype) for shape in shapes]
+        + [sem((2 * rows + 4,)), sem((2 * rows + 4,))],
+        compiler_params=pltpu.CompilerParams(vmem_limit_bytes=60 * 2**20),
+    )(*results)
+    return upd, gp, gwi, gwo, ggi.reshape(C), ggo.reshape(C)
 
 
 def solution(mesh):

time: 180 us -> 168 us (0.933)
  local copies, waits for them, and re-layouts: 6.09 us -> 0 us
  Pallas kernels: 172 us -> 166 us
    pallas_call x1 -> x2, Pallas kernels: 172 us -> 166 us  [the longest x1 163 us: on_device(): pl.pallas_call(functools.partial(kernel, rows, length), out_shape=shapes,...]
    unnamed x10 -> x0, local copies, waits for them, and re-layouts: 4.82 us -> none
where the time goes in v3:
time: 168 us; the launch traced here: 167 us
  Pallas kernels  166 us (99%)
    pallas_call x1, Pallas kernels, on_device(): pl.pallas_call(functools.partial(kernel, rows, length), out_shape=shapes,...  163 us

profile of v3, /device:TPU:1, one launch (start us, length us, event | category | flops | bytes accessed | tf_op | source)
XLA Modules:
  0.0 166.6 jit_solution(7089147335586644164)
XLA Ops:
  0.6 163.2 %shard_map.109 = (bf16[5,640,128]{2,1,0:T(8,128)(2,1)}, bf16[5,640,128]{2,1,0:T(8,128)(2,1)}, f32[128,640]{1,0:T(8,128)}, f32[128,128]{1,0:T(8,128)}, f32[1,128]{1,0:T(1,128)}, /*index=5*/f32[1,128]{1,0:T(1,128)}) custom-call(bf16[5,640,128]{2,1,0:T(8,128)(2,1)} %z_ref.1, f32[1,128]{1,0:T(1,128)} %bitcast.4, bf16[128,640]{1,0:T(8,128)(2,1)} %w_in_ref.1, ...), custom_call_target="tpu_custom_call" | custom-call | tf_op jit(solution)/shard_map/pallas_call | solution.py:649
  163.8 2.6 %shard_map.110 = (bf16[5,640,128]{2,1,0:T(8,128)(2,1)}, bf16[5,640,128]{2,1,0:T(8,128)(2,1)}, f32[128,640]{1,0:T(8,128)}, f32[128,128]{1,0:T(8,128)}, f32[1,128]{1,0:T(1,128)}, /*index=5*/f32[1,128]{1,0:T(1,128)}) custom-call(bf16[5,640,128]{2,1,0:T(8,128)(2,1)} %get-tuple-element.18.refs_0_, bf16[5,640,128]{2,1,0:T(8,128)(2,1)} %get-tuple-element.19.refs_1_, ...), custom_call_target="tpu_custom_call" | custom-call | tf_op jit(solution)/shard_map/pallas_call | solution.py:700

commit v4 on v3

--- a/solution.py
+++ b/solution.py
@@ -15,9 +15,10 @@
 GROUP = 2 * LINE
 GROWS = 16
 SIDE = 7
-ROUND = (1, 7, 2, 6, 3, 5, 4)
+ROUND = (4, 3, 5, 2, 6, 1, 7)
 CHUNKS = ((0, 1), (1, 2), (3, 2))
 ALL = range(len(CHUNKS))
+LATE = (1, 2, 0)
 
 
 def dot(a, b, dims=((1,), (0,))):
@@ -153,7 +154,7 @@
             for q in range(GROUP):
                 out[q] = mixed[q * stride : q * stride + piece, :].astype(BF)
         mine = b * 2 + core
-        for t in (0,) + ROUND:
+        for t in ROUND + (0,):
             at_b = (b + t) % LINE
             for turn in (0, 1):
                 if t == 0 and turn == 0:
@@ -201,7 +202,7 @@
             wide[...] = whole
         else:
             out[...] = whole.astype(BF).reshape(GROUP, GROUP, length)
-        for t in (0,) + ROUND:
+        for t in ROUND + (0,):
             at_b = (b + t) % LINE
             if single:
                 part = wide[pl.ds(pl.multiple_of(at_b * 2 * lot, GROUP), 2 * lot), :]
@@ -294,7 +295,7 @@
         send_rows(1, chunk)
     for block in (0, 1, 4):
         weights(block)
-    for chunk in ALL:
+    for chunk in LATE:
         for row in chunk_rows(chunk):
             proj = dot(w_in_t[: 2 * C, :], normed[row])
             s_l[row] = sigmoid(proj[C:])
@@ -339,14 +340,14 @@
         relay_rows(1, chunk)
     for row in range(rows):
         s_g[row] = sigmoid(dot(w_in_t[4 * C :, :], normed[row]))
-    for chunk in ALL:
+    for chunk in LATE:
         relay_rows(0, chunk)
     for row in range(rows):
         cot_t[row] = dot(eye, cot_ref[row], NT)
     for chunk in ALL:
         take_channel(1, chunk, turned_m)
     right_m[...] = dot(order[...], turned_m[...]).astype(BF)
-    for chunk in ALL:
+    for chunk in LATE:
         take_channel(0, chunk, left_m)
         send_channel(2, chunk, dot(of(left_m, chunk), right_m[...], NT))
 
@@ -385,25 +386,26 @@
     def right_back(chunk):
         send_channel(5, chunk, dot(of(turned_m, chunk), left_m[...]))
 
-    relay_channel(2, 0)
-    relay_channel(2, 1)
-    middle(0)
-    relay_channel(2, 2)
-    middle(1)
-    relay_rows(3, 0)
-    middle(2)
-    relay_rows(3, 1)
-    left_back(0)
-    relay_rows(3, 2)
-    left_back(1)
-    left_back(2)
-    relay_channel(4, 0)
+    c0, c1, c2 = LATE
+    relay_channel(2, c0)
+    relay_channel(2, c1)
+    middle(c0)
+    relay_channel(2, c2)
+    middle(c1)
+    relay_rows(3, c0)
+    middle(c2)
+    relay_rows(3, c1)
+    left_back(c0)
+    relay_rows(3, c2)
+    left_back(c1)
+    left_back(c2)
+    relay_channel(4, c0)
     turned_m[...] = dot(order_t[...], dprod_m[...], NT).astype(BF)
-    right_back(0)
-    relay_channel(4, 1)
-    right_back(1)
-    relay_channel(4, 2)
-    right_back(2)
+    right_back(c0)
+    relay_channel(4, c1)
+    right_back(c1)
+    relay_channel(4, c2)
+    right_back(c2)
     gg_out = gg_parts[0] + gg_parts[1] + gg_parts[2]
     gw = jnp.zeros((C, C), FL)
     gw_gate = jnp.zeros((C, C), FL)
@@ -457,17 +459,17 @@
 
     total = jnp.zeros((C, 2 * C), FL)
     write_update(range(0, 2))
-    total = factor_back(0, 0, total)
-    relay_channel(5, 0)
-    total = factor_back(0, 1, total)
-    relay_channel(5, 1)
+    total = factor_back(0, c0, total)
+    relay_channel(5, c0)
+    total = factor_back(0, c1, total)
+    relay_channel(5, c1)
     write_update(range(2, rows))
-    total = factor_back(0, 2, total)
+    total = factor_back(0, c2, total)
     weights_back(0, total)
-    relay_channel(5, 2)
+    relay_channel(5, c2)
     total = jnp.zeros((C, 2 * C), FL)
     gg_in = jnp.zeros((C, C), FL)
-    for chunk in ALL:
+    for chunk in LATE:
         total = factor_back(1, chunk, total)
         for row in chunk_rows(chunk):
             d_normed = dot(w_in_p[...], d_proj[row])
@@ -475,7 +477,7 @@
             both = d_normed * zhat[row]
             for tile in range(tiles):
                 gg_in = gg_in + both[:, tile * C : (tile + 1) * C]
-        if chunk < 2:
+        if chunk != c2:
             write_rows(chunk_rows(chunk))
     weights_back(1, total)
 
@@ -508,6 +510,7 @@
     def some(ref, count, on_send, on_recv):
         return remote(ref.at[pl.ds(0, count)], ref.at[pl.ds(0, count)], on_send, on_recv, other)
 
+    write_rows(chunk_rows(c2))
     mine = b * 2 + core
 
     @pl.when(in_a)
@@ -515,7 +518,7 @@
         g_recv[a] = g_send[a]
         some(g_recv, LINE - 1, g_sems.at[0], g_sems.at[1]).wait_recv()
         h_send[...] = jnp.sum(g_recv[...].astype(FL), axis=0).astype(BF)
-        for t in (0,) + ROUND:
+        for t in ROUND + (0,):
             at_b = (b + t) % LINE
             for turn in (0, 1):
                 if t == 0 and turn == 0:
@@ -532,7 +535,6 @@
                         device(a, at_b, at_core),
                     ).start()
 
-    write_rows(range(3, 4))
 
     @pl.when(owner)
     def _():
@@ -546,7 +548,6 @@
             ).start()
         c_recv[b] = o_send[...]
 
-    write_rows(range(4, rows))
 
     @pl.when(in_a)
     def _():

time: 168 us -> 156 us (0.929)
  Pallas kernels: 166 us -> 155 us
    pallas_call x1, Pallas kernels: 163 us -> 152 us  [on_device(): pl.pallas_call(functools.partial(kernel, rows, length), out_shape=shapes,...]
where the time goes in v4:
time: 156 us
  Pallas kernels  155 us (99%)
    pallas_call x1, Pallas kernels, on_device(): pl.pallas_call(functools.partial(kernel, rows, length), out_shape=shapes,...  152 us

profile of v4, /device:TPU:1, one launch (start us, length us, event | category | flops | bytes accessed | tf_op | source)
XLA Modules:
  0.0 155.5 jit_solution(4213494771432398585)
XLA Ops:
  0.6 152.2 %shard_map.109 = (bf16[5,640,128]{2,1,0:T(8,128)(2,1)}, bf16[5,640,128]{2,1,0:T(8,128)(2,1)}, f32[128,640]{1,0:T(8,128)}, f32[128,128]{1,0:T(8,128)}, f32[1,128]{1,0:T(1,128)}, /*index=5*/f32[1,128]{1,0:T(1,128)}) custom-call(bf16[5,640,128]{2,1,0:T(8,128)(2,1)} %z_ref.1, f32[1,128]{1,0:T(1,128)} %bitcast.4, bf16[128,640]{1,0:T(8,128)(2,1)} %w_in_ref.1, ...), custom_call_target="tpu_custom_call" | custom-call | tf_op jit(solution)/shard_map/pallas_call | solution.py:650
  152.8 2.6 %shard_map.110 = (bf16[5,640,128]{2,1,0:T(8,128)(2,1)}, bf16[5,640,128]{2,1,0:T(8,128)(2,1)}, f32[128,640]{1,0:T(8,128)}, f32[128,128]{1,0:T(8,128)}, f32[1,128]{1,0:T(1,128)}, /*index=5*/f32[1,128]{1,0:T(1,128)}) custom-call(bf16[5,640,128]{2,1,0:T(8,128)(2,1)} %get-tuple-element.18.refs_0_, bf16[5,640,128]{2,1,0:T(8,128)(2,1)} %get-tuple-element.19.refs_1_, ...), custom_call_target="tpu_custom_call" | custom-call | tf_op jit(solution)/shard_map/pallas_call | solution.py:701

commit v5 on v4

--- a/solution.py
+++ b/solution.py
@@ -398,8 +398,8 @@
     left_back(c0)
     relay_rows(3, c2)
     left_back(c1)
+    relay_channel(4, c0)
     left_back(c2)
-    relay_channel(4, c0)
     turned_m[...] = dot(order_t[...], dprod_m[...], NT).astype(BF)
     right_back(c0)
     relay_channel(4, c1)
@@ -463,10 +463,10 @@
     relay_channel(5, c0)
     total = factor_back(0, c1, total)
     relay_channel(5, c1)
+    total = factor_back(0, c2, total)
+    relay_channel(5, c2)
+    weights_back(0, total)
     write_update(range(2, rows))
-    total = factor_back(0, c2, total)
-    weights_back(0, total)
-    relay_channel(5, c2)
     total = jnp.zeros((C, 2 * C), FL)
     gg_in = jnp.zeros((C, C), FL)
     for chunk in LATE:

time: 156 us -> 155 us (level)
  Pallas kernels: 155 us -> 153 us
    pallas_call x1, Pallas kernels: 152 us -> 150 us  [on_device(): pl.pallas_call(functools.partial(kernel, rows, length), out_shape=shapes,...]
where the time goes in v5:
time: 155 us; the launch traced here: 154 us
  Pallas kernels  153 us (99%)
    pallas_call x1, Pallas kernels, on_device(): pl.pallas_call(functools.partial(kernel, rows, length), out_shape=shapes,...  150 us

profile of v5, /device:TPU:1, one launch (start us, length us, event | category | flops | bytes accessed | tf_op | source)
XLA Modules:
  0.0 153.7 jit_solution(5187403988143162372)
XLA Ops:
  0.6 150.3 %shard_map.109 = (bf16[5,640,128]{2,1,0:T(8,128)(2,1)}, bf16[5,640,128]{2,1,0:T(8,128)(2,1)}, f32[128,640]{1,0:T(8,128)}, f32[128,128]{1,0:T(8,128)}, f32[1,128]{1,0:T(1,128)}, /*index=5*/f32[1,128]{1,0:T(1,128)}) custom-call(bf16[5,640,128]{2,1,0:T(8,128)(2,1)} %z_ref.1, f32[1,128]{1,0:T(1,128)} %bitcast.4, bf16[128,640]{1,0:T(8,128)(2,1)} %w_in_ref.1, ...), custom_call_target="tpu_custom_call" | custom-call | tf_op jit(solution)/shard_map/pallas_call | solution.py:650
  150.9 2.6 %shard_map.110 = (bf16[5,640,128]{2,1,0:T(8,128)(2,1)}, bf16[5,640,128]{2,1,0:T(8,128)(2,1)}, f32[128,640]{1,0:T(8,128)}, f32[128,128]{1,0:T(8,128)}, f32[1,128]{1,0:T(1,128)}, /*index=5*/f32[1,128]{1,0:T(1,128)}) custom-call(bf16[5,640,128]{2,1,0:T(8,128)(2,1)} %get-tuple-element.18.refs_0_, bf16[5,640,128]{2,1,0:T(8,128)(2,1)} %get-tuple-element.19.refs_1_, ...), custom_call_target="tpu_custom_call" | custom-call | tf_op jit(solution)/shard_map/pallas_call | solution.py:701

commit v6 on v5

--- a/solution.py
+++ b/solution.py
@@ -338,11 +338,10 @@
 
     for chunk in ALL:
         relay_rows(1, chunk)
-    for row in range(rows):
-        s_g[row] = sigmoid(dot(w_in_t[4 * C :, :], normed[row]))
     for chunk in LATE:
         relay_rows(0, chunk)
     for row in range(rows):
+        s_g[row] = sigmoid(dot(w_in_t[4 * C :, :], normed[row]))
         cot_t[row] = dot(eye, cot_ref[row], NT)
     for chunk in ALL:
         take_channel(1, chunk, turned_m)

time: 155 us -> 155 us (level)
  no operation moved by 1% of the time
where the time goes in v6:
time: 155 us; the launch traced here: 154 us
  Pallas kernels  153 us (99%)
    pallas_call x1, Pallas kernels, on_device(): pl.pallas_call(functools.partial(kernel, rows, length), out_shape=shapes,...  151 us

profile of v6, /device:TPU:1, one launch (start us, length us, event | category | flops | bytes accessed | tf_op | source)
XLA Modules:
  0.0 153.9 jit_solution(8925957815031445985)
XLA Ops:
  0.6 150.5 %shard_map.109 = (bf16[5,640,128]{2,1,0:T(8,128)(2,1)}, bf16[5,640,128]{2,1,0:T(8,128)(2,1)}, f32[128,640]{1,0:T(8,128)}, f32[128,128]{1,0:T(8,128)}, f32[1,128]{1,0:T(1,128)}, /*index=5*/f32[1,128]{1,0:T(1,128)}) custom-call(bf16[5,640,128]{2,1,0:T(8,128)(2,1)} %z_ref.1, f32[1,128]{1,0:T(1,128)} %bitcast.4, bf16[128,640]{1,0:T(8,128)(2,1)} %w_in_ref.1, ...), custom_call_target="tpu_custom_call" | custom-call | tf_op jit(solution)/shard_map/pallas_call | solution.py:649
  151.1 2.6 %shard_map.110 = (bf16[5,640,128]{2,1,0:T(8,128)(2,1)}, bf16[5,640,128]{2,1,0:T(8,128)(2,1)}, f32[128,640]{1,0:T(8,128)}, f32[128,128]{1,0:T(8,128)}, f32[1,128]{1,0:T(1,128)}, /*index=5*/f32[1,128]{1,0:T(1,128)}) custom-call(bf16[5,640,128]{2,1,0:T(8,128)(2,1)} %get-tuple-element.18.refs_0_, bf16[5,640,128]{2,1,0:T(8,128)(2,1)} %get-tuple-element.19.refs_1_, ...), custom_call_target="tpu_custom_call" | custom-call | tf_op jit(solution)/shard_map/pallas_call | solution.py:700
